TPU v7x, 512 devices: a whole 4x8x8 slice. The times are simulated.
512 devices in a mesh: mem: 16 (over z, core), reg: 32 (over y, x).
Axes of the slice: x: 4, y: 8, z: 8, core: 2. Of those that a mesh axis runs over, the one named last changes fastest.
Arguments:
- starting_sample_set: float32 [80, 4, 128, 1024], P('mem', None, 'reg'), may hold values from -6 to 6
- block_owner: int32 [3], replicated, may hold values from 0 to 31, as said below
- obs_location: int32 [3, 512], replicated, may hold values from 0 to 16383
- taper_pairs: int32 [3, 2], replicated, may hold values from 64 to 256, as said below
- obs_values: float32 [3, 512], replicated, may hold values from -6 to 6
- obs_noise: float32 [3, 80, 512], replicated, may hold values from -5 to 5
- obs_variance: float32 [3, 512], replicated, may hold values from 0.2 to 2
Outputs:
- analysis: float32 [80, 524288], P(None, ('reg', 'mem'))
Inputs may be any that keep to these rules, and one draw needn't show every extreme that they name: `block_owner`: the owners of the blocks are distinct regions. `taper_pairs`: column 0 is a row half-width from 64 to 128 and column 1 a column half-width from 64 to 256; each of these four ends is taken by some block in every draw.
All inputs are finite; a program needn't handle non-finite values.
Results may differ from a plain program's by a relative error of at most 0.00019.
Values sent between devices are 32-bit elements; how exact they have to be, the bound alone decides.
No kernel may reach another device: no remote copies, remote signals or barrier semaphores. Data moves between devices by JAX's collectives and lax.ppermute only.
A program may use at most 64 MiB of HBM per device.

v0:
```python
import jax
import jax.numpy as jnp
from jax import lax
from jax.sharding import PartitionSpec as P

STEPS = 4


mixing = 0.1
courant = 0.05
gravity = 1.0
rotation = 0.02
highest = lax.Precision.HIGHEST


def with_halo(cells, sides, width):
    for axis, dim in sides:
        count = lax.axis_size(axis)
        head = lax.slice_in_dim(cells, 0, width, axis=dim)
        tail = lax.slice_in_dim(cells, cells.shape[dim] - width, cells.shape[dim], axis=dim)
        cells = jnp.concatenate(
            [
                lax.ppermute(tail, axis, [(i, (i + 1) % count) for i in range(count)]),
                cells,
                lax.ppermute(head, axis, [((i + 1) % count, i) for i in range(count)]),
            ],
            axis=dim,
        )
    return cells


def spread_2(block, axis, holder):
    block = jnp.where(lax.axis_index(axis) == holder, block, jnp.zeros_like(block))
    return lax.psum(block, axis)


def advance(center, row_above, row_below, col_west, col_east):
    smooth = (1.0 - mixing) * center + mixing * 0.25 * (row_above + row_below + col_west + col_east)
    col_diff = col_east - col_west
    row_diff = row_below - row_above
    speed_u = center[:, 1:2]
    speed_v = center[:, 2:3]
    carried = speed_u * col_diff + speed_v * row_diff
    net_flux = (
        (1.0 + col_east[:, 0]) * col_east[:, 1]
        - (1.0 + col_west[:, 0]) * col_west[:, 1]
        + (1.0 + row_below[:, 0]) * row_below[:, 2]
        - (1.0 + row_above[:, 0]) * row_above[:, 2]
    )
    new_depth = smooth[:, 0] - courant * net_flux
    new_east = (
        smooth[:, 1]
        - courant * (carried[:, 1] + gravity * col_diff[:, 0])
        + rotation * center[:, 2]
    )
    new_north = (
        smooth[:, 2]
        - courant * (carried[:, 2] + gravity * row_diff[:, 0])
        - rotation * center[:, 1]
    )
    new_tracer = smooth[:, 3] - courant * carried[:, 3]
    return jnp.stack([new_depth, new_east, new_north, new_tracer], axis=1)


def advance_rows(padded):
    center = padded[:, :, 1:-1]
    return advance(
        center,
        padded[:, :, :-2],
        padded[:, :, 2:],
        jnp.roll(center, 1, axis=3),
        jnp.roll(center, -1, axis=3),
    )


def taper_weight(
    row_first, col_first, row_second, col_second, widths, meridional_extent, lateral_extent
):
    gap_row = jnp.abs(row_first[:, None] - row_second[None, :])
    gap_row = jnp.minimum(gap_row, meridional_extent - gap_row)
    gap_col = jnp.abs(col_first[:, None] - col_second[None, :])
    gap_col = jnp.minimum(gap_col, lateral_extent - gap_col)
    weight_row = jnp.maximum(0.0, 1.0 - gap_row.astype(jnp.float32) / widths[0].astype(jnp.float32))
    weight_col = jnp.maximum(0.0, 1.0 - gap_col.astype(jnp.float32) / widths[1].astype(jnp.float32))
    return weight_row * weight_col


def gain_weights(
    predicted, obs_row, obs_col, widths, variance, values, noise, meridional_extent, lateral_extent
):
    realization_array = predicted.shape[0]
    obs_anomaly = predicted - jnp.mean(predicted, axis=0, keepdims=True)
    spread = lax.dot_general(
        obs_anomaly, obs_anomaly, (((0,), (0,)), ((), ())), precision=highest
    ) / (realization_array - 1)
    innovation_cov = taper_weight(
        obs_row, obs_col, obs_row, obs_col, widths, meridional_extent, lateral_extent
    ) * spread + jnp.diag(variance)
    factor = jnp.linalg.cholesky(innovation_cov)
    misfit = values[None, :] + noise - predicted
    weights = jax.scipy.linalg.cho_solve((factor, True), misfit.T).T
    return (obs_anomaly, weights)


def assimilate(
    state_rows,
    var_row,
    var_col,
    obs_anomaly,
    weights,
    obs_row,
    obs_col,
    widths,
    meridional_extent,
    lateral_extent,
):
    realization_array = state_rows.shape[0]
    centered = state_rows - jnp.mean(state_rows, axis=0, keepdims=True)
    cross_cov = lax.dot_general(
        centered, obs_anomaly, (((0,), (0,)), ((), ())), precision=highest
    ) / (realization_array - 1)
    tapered = (
        taper_weight(var_row, var_col, obs_row, obs_col, widths, meridional_extent, lateral_extent)
        * cross_cov
    )
    return state_rows + lax.dot_general(
        weights, tapered, (((1,), (1,)), ((), ())), precision=highest
    )


def shards(
    starting_sample_set, block_owner, obs_location, taper_pairs, obs_values, obs_noise, obs_variance
):
    mem_dev, gridded_quantity_array, shard_rows, grid_cols = starting_sample_set.shape
    subdomain_sequence = lax.axis_size("reg")
    region = lax.axis_index("reg")
    mem_index = lax.axis_index("mem")
    meridional_extent = shard_rows * subdomain_sequence
    current_model_vector = starting_sample_set
    for counter in range(STEPS):
        padded = with_halo(current_model_vector, (("reg", 2),), 1)
        current_model_vector = advance_rows(padded)
    members_all = lax.all_to_all(
        current_model_vector.reshape(mem_dev, gridded_quantity_array * shard_rows * grid_cols),
        "mem",
        split_axis=1,
        concat_axis=0,
        tiled=True,
    )
    vars_dev = members_all.shape[1]
    var_index = mem_index * vars_dev + jnp.arange(vars_dev, dtype=jnp.int32)
    var_row = region * shard_rows + var_index // grid_cols % shard_rows
    var_col = var_index % grid_cols
    for block_id in range(obs_location.shape[0]):
        owner_reg = block_owner[block_id]
        obs_cell = obs_location[block_id]
        widths = taper_pairs[block_id]
        obs_row = owner_reg * shard_rows + obs_cell // grid_cols % shard_rows
        obs_col = obs_cell % grid_cols
        held_here = jnp.logical_and(region == owner_reg, obs_cell // vars_dev == mem_index)
        picked = (
            jnp.take(members_all, obs_cell % vars_dev, axis=1)
            * held_here.astype(jnp.float32)[None, :]
        )

        def gain_solve(predicted):
            return gain_weights(
                predicted,
                obs_row,
                obs_col,
                widths,
                obs_variance[block_id],
                obs_values[block_id],
                obs_noise[block_id],
                meridional_extent,
                grid_cols,
            )

        predicted = lax.psum(picked, "mem")

        def no_gain(predicted):
            return (jnp.zeros_like(predicted), jnp.zeros_like(predicted))

        obs_anomaly, weights = lax.cond(region == owner_reg, gain_solve, no_gain, predicted)
        obs_anomaly, weights = (
            spread_2(obs_anomaly, "reg", owner_reg),
            spread_2(weights, "reg", owner_reg),
        )
        members_all = assimilate(
            members_all,
            var_row,
            var_col,
            obs_anomaly,
            weights,
            obs_row,
            obs_col,
            widths,
            meridional_extent,
            grid_cols,
        )
    return members_all


def solution(mesh):
    return jax.shard_map(
        shards,
        mesh=mesh,
        in_specs=(P("mem", None, "reg", None), P(), P(), P(), P(), P(), P()),
        out_specs=P(None, ("reg", "mem")),
        check_vma=False,
    )
```

profile of v0, /device:TPU:1, one launch (start us, length us, event | category | flops | bytes accessed | tf_op | source)
XLA Modules:
  0.0 1376.4 jit_solution(2441368042850046456)
XLA Ops:
  6.5 1.3 fusion.409
  7.8 8.1 collective-permute-start.1
  16.0 1.9 collective-permute-start
  17.9 1.4 fusion.413
  22.9 1.5 fusion.366
  24.4 0.9 fusion.411
  25.3 0.9 slice_bitcast_fusion.37
  26.2 1.3 fusion.410
  32.2 6.7 collective-permute-start.3
  38.9 1.9 collective-permute-start.2
  40.9 6.5 collective-permute-done.2
  49.0 1.9 collective-permute-start.5
  50.9 3.4 collective-permute-start.4
  54.4 5.0 collective-permute-done.4
  61.1 1.9 collective-permute-start.7
  63.0 3.4 collective-permute-start.6
  66.5 5.0 collective-permute-done.6
  72.8 1.0 copy.37
  73.8 15.3 %all-to-all-start = ((f32[5,16,1024]{2,0,1:T(8,128)}), f32[5,16,1024]{2,0,1:T(8,128)S(1)}, u32[]{:S(2)}, u32[]{:S(2)}) async-start(f32[5,16,1024]{2,0,1:T(8,128)} %bitcast.8), calls=%async_computation | async-start | bytes 1048576 | tf_op jit(solution)/shard_map/all_to_all | solution.py:143
  90.5 15.9 %all-to-all-done = f32[5,16,1024]{2,0,1:T(8,128)S(1)} async-done(((f32[5,16,1024]{2,0,1:T(8,128)}), f32[5,16,1024]{2,0,1:T(8,128)S(1)}, u32[]{:S(2)}, u32[]{:S(2)}) %all-to-all-start) | async-done | bytes 327712 | tf_op jit(solution)/shard_map/all_to_all | solution.py:143
  106.7 1.0 gather_fusion
  107.7 0.9 bitcast_multiply_fusion.2
  108.7 105.7 %all-reduce.11.cloned.1.call-done = f32[80,512]{0,1:T(8,128)} async-done(((f32[80,512]{0,1:T(8,128)}), f32[80,512]{0,1:T(8,128)}) %all-reduce.11.cloned.1.call-update) | async-done | bytes 163856 | tf_op jit(solution)/shard_map/psum | solution.py:179
  214.5 150.5 %conditional.3 = (f32[80,512]{1,0:T(8,128)S(1)}, f32[80,512]{1,0:T(8,128)S(1)}) conditional(s32[]{:T(128)} %convert_element_type.123, () %tuple.32, (f32[80,512]{0,1:T(8,128)}, s32[]{:T(128)}, s32[3,2]{0,1:T(2,128)S(1)}, s32[512]{0:T(512)S(1)}, f32[3,512]{1,0:T(4,128)S(1)}, /*index=5*/f32[3,512]{1,0:T(4,128)S(1)}, ...), branch_computations={%region_1.3_spmd, %region_2.15_spmd.clone.clone} | conditional | flops 977134080 | bytes 23656324 | solution.py:184
  216.6 1.1 reduce_sum.60
  217.7 1.1 copy.39
  218.8 0.9 fusion.19
  219.7 1.9 fusion.1
  222.2 1.0 copy-done.1
  223.2 11.7 cholesky.590
  234.9 9.8 custom-call.45
  244.9 1.2 constant_dynamic-update-slice_fusion.3
  246.1 1.3 convolution_subtract_fusion
  247.4 12.1 cholesky.605
  261.5 9.8 custom-call.46
  271.6 1.3 convolution_subtract_fusion.1
  272.9 11.7 cholesky.622
  286.1 9.8 custom-call.47
  296.1 1.2 convolution_subtract_fusion.2
  297.3 11.9 cholesky.635
  310.5 10.5 while.9
  311.2 2.0 bitcast_dynamic-update-slice_fusion.8
  313.8 2.0 bitcast_dynamic-update-slice_fusion.8
  316.4 2.0 bitcast_dynamic-update-slice_fusion.8
  319.1 2.0 bitcast_dynamic-update-slice_fusion.8
  321.0 40.1 %custom-call.48 = f32[4,128,128]{1,2,0:T(8,128)S(1)} custom-call(f32[4,128,128]{2,1,0:T(8,128)} %get-tuple-element.325), custom_call_target="InvertDiagBlocksLowerTriangular" | custom-call | tf_op jit(solution)/shard_map/cond/branch_1_fun/jit(_cho_solve)/triangular_solve | solution.py:101
  365.0 0.7 broadcast_select_fusion.4
  365.9 144.4 %all-reduce.21.cloned.1.call-done = (f32[80,512]{1,0:T(8,128)}, f32[80,512]{1,0:T(8,128)}) async-done(((f32[80,512]{1,0:T(8,128)}, f32[80,512]{1,0:T(8,128)}), (f32[80,512]{1,0:T(8,128)}, f32[80,512]{1,0:T(8,128)})) %all-reduce.21.cloned.1.call-update) | async-done | bytes 327696 | tf_op jit(solution)/shard_map/psum | solution.py:34
  510.3 2.8 fusion.267
  513.1 3.8 fusion.414
  517.1 1.0 gather_fusion.1
  518.2 0.9 bitcast_multiply_fusion.1
  520.4 115.3 %all-reduce.13.cloned.1.call-done = f32[80,512]{0,1:T(8,128)} async-done(((f32[80,512]{0,1:T(8,128)}), f32[80,512]{0,1:T(8,128)}) %all-reduce.13.cloned.1.call-update) | async-done | bytes 163856 | tf_op jit(solution)/shard_map/psum | solution.py:179
  635.7 5.4 conditional.4
  642.6 294.3 %all-reduce.19.cloned.1.call-done = (f32[80,512]{1,0:T(8,128)}, f32[80,512]{1,0:T(8,128)}) async-done(((f32[80,512]{1,0:T(8,128)}, f32[80,512]{1,0:T(8,128)}), (f32[80,512]{1,0:T(8,128)}, f32[80,512]{1,0:T(8,128)})) %all-reduce.19.cloned.1.call-update) | async-done | bytes 327696 | tf_op jit(solution)/shard_map/psum | solution.py:34
  936.9 2.8 fusion.265
  939.8 3.8 fusion.415
  943.8 1.0 gather_fusion.2
  944.8 0.9 bitcast_multiply_fusion
  945.8 116.5 %all-reduce.15.cloned.1.call-done = f32[80,512]{0,1:T(8,128)} async-done(((f32[80,512]{0,1:T(8,128)}), f32[80,512]{0,1:T(8,128)}) %all-reduce.15.cloned.1.call-update) | async-done | bytes 163856 | tf_op jit(solution)/shard_map/psum | solution.py:179
  1062.3 4.5 conditional.5
  1069.6 292.2 %all-reduce.17.cloned.1.call-done = (f32[80,512]{1,0:T(8,128)}, f32[80,512]{1,0:T(8,128)}) async-done(((f32[80,512]{1,0:T(8,128)}, f32[80,512]{1,0:T(8,128)}), (f32[80,512]{1,0:T(8,128)}, f32[80,512]{1,0:T(8,128)})) %all-reduce.17.cloned.1.call-update) | async-done | bytes 327696 | tf_op jit(solution)/shard_map/psum | solution.py:34
  1361.9 2.8 fusion.263
  1364.7 4.7 fusion.225
  (166 shorter events, 25.5 us)
Async XLA Ops:
  6.5 24.1 %copy-start = (f32[5,4,4,1024]{3,2,1,0:T(4,128)S(1)}, f32[5,4,4,1024]{3,2,1,0:T(4,128)}, u32[]{:S(2)}) copy-start(f32[5,4,4,1024]{3,2,1,0:T(4,128)} %param.18) | copy-start | bytes 983044
  6.5 23.4 %copy-start.6 = (s32[3,2]{0,1:T(2,128)S(1)}, s32[3,2]{0,1:T(2,128)}, u32[]{:S(2)}) copy-start(s32[3,2]{0,1:T(2,128)} %param.21) | copy-start | bytes 76
  7.8 22.8 %collective-permute-start.1 = (f32[5,4,1,1024]{3,2,1,0:T(1,128)S(1)}, f32[5,4,1,1024]{3,2,1,0:T(1,128)S(1)}, u32[]{:S(2)}, u32[]{:S(2)}) collective-permute-start(f32[5,4,1,1024]{3,2,1,0:T(1,128)S(1)} %get-tuple-element.563), channel_id=1, source_target_pairs={{1,0},{2,1},{3,2},{4,3},{5,4},{6,5},{7,6},{8,7},{9,8},{10,9},{11,1... | collective-permute-start | bytes 245768 | tf_op jit(solution)/shard_map/ppermute | solution.py:25
  16.0 14.7 %collective-permute-start = (f32[5,4,1,1024]{3,2,1,0:T(1,128)S(1)}, f32[5,4,1,1024]{3,2,1,0:T(1,128)S(1)}, u32[]{:S(2)}, u32[]{:S(2)}) collective-permute-start(f32[5,4,1,1024]{3,2,1,0:T(1,128)S(1)} %get-tuple-element.564), channel_id=1, source_target_pairs={{0,1},{1,2},{2,3},{3,4},{4,5},{5,6},{6,7},{7,8},{8,9},{9,10},{10,1... | collective-permute-start | bytes 245768 | tf_op jit(solution)/shard_map/ppermute | solution.py:23
  32.2 8.7 collective-permute-start.3
  38.9 8.5 collective-permute-start.2
  49.0 5.4 collective-permute-start.5
  50.9 8.5 collective-permute-start.4
  61.1 5.4 collective-permute-start.7
  63.0 8.5 collective-permute-start.6
  73.8 32.6 %all-to-all-start = ((f32[5,16,1024]{2,0,1:T(8,128)}), f32[5,16,1024]{2,0,1:T(8,128)S(1)}, u32[]{:S(2)}, u32[]{:S(2)}) async-start(f32[5,16,1024]{2,0,1:T(8,128)} %bitcast.8), calls=%async_computation | async-start | bytes 1048576 | tf_op jit(solution)/shard_map/all_to_all | solution.py:143
  89.1 125.4 %copy-start.7 = (f32[3,512]{1,0:T(4,128)S(1)}, f32[3,512]{1,0:T(4,128)}, u32[]{:S(2)}) copy-start(f32[3,512]{1,0:T(4,128)} %param.24) | copy-start | bytes 18436
  89.1 125.4 %copy-start.8 = (f32[3,512]{1,0:T(4,128)S(1)}, f32[3,512]{1,0:T(4,128)}, u32[]{:S(2)}) copy-start(f32[3,512]{1,0:T(4,128)} %param.22) | copy-start | bytes 18436
  89.1 125.4 %all-reduce.11.cloned.1.call-start = ((), (), s32[]{:S(2)}) async-start(), calls=%async_computation.1 | async-start | bytes 524288 | tf_op jit(solution)/shard_map/psum | solution.py:179
  108.7 401.6 %all-reduce.21.cloned.1.call-start = ((), (), s32[]{:S(2)}) async-start(), calls=%async_computation.6 | async-start | bytes 655360 | tf_op jit(solution)/shard_map/psum | solution.py:34
  219.7 1.9 copy-start.4
  222.2 1.0 copy-start.1
  310.5 54.3 %copy-start.5 = (f32[80,512]{1,0:T(8,128)S(1)}, f32[80,512]{1,0:T(8,128)}, u32[]{:S(2)}) copy-start(f32[80,512]{1,0:T(8,128)} %copy-done.4) | copy-start | bytes 491524 | tf_op jit(solution)/shard_map/cond
  365.0 148.1 %copy-start.13 = (s32[1,512]{1,0:T(1,128)S(1)}, s32[1,512]{1,0:T(1,128)}, u32[]{:S(2)}) copy-start(s32[1,512]{1,0:T(1,128)} %get-tuple-element.574) | copy-start | bytes 6148
  365.0 148.1 %copy-start.15 = (s32[1,512]{1,0:T(1,128)S(1)}, s32[1,512]{1,0:T(1,128)}, u32[]{:S(2)}) copy-start(s32[1,512]{1,0:T(1,128)} %and_select_fusion.6) | copy-start | bytes 6148
  365.8 269.9 %all-reduce.13.cloned.1.call-start = ((), (), s32[]{:S(2)}) async-start(), calls=%async_computation.2 | async-start | bytes 524288 | tf_op jit(solution)/shard_map/psum | solution.py:179
  510.3 2.8 copy-start.16
  516.9 1.3 copy-start.10
  519.1 417.8 %all-reduce.19.cloned.1.call-start = ((), (), s32[]{:S(2)}) async-start(), calls=%async_computation.5 | async-start | bytes 655360 | tf_op jit(solution)/shard_map/psum | solution.py:34
  641.1 298.6 %copy-start.12 = (s32[1,512]{1,0:T(1,128)S(1)}, s32[1,512]{1,0:T(1,128)}, u32[]{:S(2)}) copy-start(s32[1,512]{1,0:T(1,128)} %get-tuple-element.571) | copy-start | bytes 6148
  641.1 298.6 %copy-start.14 = (s32[1,512]{1,0:T(1,128)S(1)}, s32[1,512]{1,0:T(1,128)}, u32[]{:S(2)}) copy-start(s32[1,512]{1,0:T(1,128)} %and_select_fusion.3) | copy-start | bytes 6148
  642.5 419.8 %all-reduce.15.cloned.1.call-start = ((), (), s32[]{:S(2)}) async-start(), calls=%async_computation.3 | async-start | bytes 524288 | tf_op jit(solution)/shard_map/psum | solution.py:179
  936.9 2.8 copy-start.18
  943.6 1.3 copy-start.9
  945.8 416.1 %all-reduce.17.cloned.1.call-start = ((), (), s32[]{:S(2)}) async-start(), calls=%async_computation.4 | async-start | bytes 655360 | tf_op jit(solution)/shard_map/psum | solution.py:34
  1066.9 297.8 %copy-start.11 = (s32[1,512]{1,0:T(1,128)S(1)}, s32[1,512]{1,0:T(1,128)}, u32[]{:S(2)}) copy-start(s32[1,512]{1,0:T(1,128)} %get-tuple-element.430) | copy-start | bytes 6148
  1361.9 2.8 copy-start.17
Sparse Core Ops, SparseCore 0:
  108.8 105.6 all-reduce.10
  365.9 144.3 all-reduce.20
  519.2 116.4 all-reduce.12
  642.7 294.2 all-reduce.18
  945.9 116.4 all-reduce.14
  1068.4 293.3 all-reduce.16
where the time goes:
time: 1390 us; the launch traced here: 1380 us
  waiting for transfers between devices  1100 us (79%)
  other arithmetic  137 us (10%)
  starting transfers between devices  44.8 us (3%)
  matrix products  31.4 us (2%)
  local copies, waits for them, and re-layouts  28.2 us (2%)
  between operations  21.8 us (2%)
    psum x3, waiting for transfers between devices, spread_2(): return lax.psum(block, axis)  731 us
    psum x3, waiting for transfers between devices, shards(): predicted = lax.psum(picked, 'mem')  338 us
    another operation x14, other arithmetic, gain_weights(): factor = jnp.linalg.cholesky(innovation_cov)  79 us
    another operation x4, other arithmetic, gain_weights(): weights = jax.scipy.linalg.cho_solve((factor, True), misfit.T).T  40.3 us
  transfers between devices with their start and end apart: 15, of which 10 were waited for; matrix products, arithmetic and copies ran while one was open for 1% of the time, Pallas kernels for 0%

commit v1 on v0

v1 whole, which is shorter than its diff:
```python
import jax
import jax.numpy as jnp
from jax import lax
from jax.experimental import pallas as pl
from jax.experimental.pallas import tpu as pltpu
from jax.sharding import PartitionSpec as P

STEPS = 4
MIX = 0.1
COURANT = 0.05
ROTATION = 0.02
LANES = 128
GROUP = 8
highest = lax.Precision.HIGHEST
f32 = jnp.float32
bf16 = jnp.bfloat16

vmem = pl.BlockSpec(memory_space=pltpu.VMEM)
smem = pl.BlockSpec(memory_space=pltpu.SMEM)
params = pltpu.CompilerParams(vmem_limit_bytes=48 * 1024 * 1024)


def dot_exact(a, b):
    return lax.dot_general(
        a, b, (((1,), (0,)), ((), ())), precision=highest, preferred_element_type=f32
    )


def dot_bf16(a, b):
    return lax.dot_general(a, b, (((1,), (0,)), ((), ())), preferred_element_type=f32)


def halves(x):
    hi = x.astype(bf16)
    return hi, (x - hi.astype(f32)).astype(bf16)


def thirds(x):
    hi = x.astype(bf16)
    rest = x - hi.astype(f32)
    mid = rest.astype(bf16)
    return hi, mid, (rest - mid.astype(f32)).astype(bf16)


def dot_split(a, b):
    a_hi, a_lo = halves(a)
    b_hi, b_lo = halves(b)
    return dot_bf16(
        jnp.concatenate([a_hi, a_hi, a_lo], axis=1), jnp.concatenate([b_hi, b_lo, b_hi], axis=0)
    )


def tree_sum(terms):
    terms = list(terms)
    while len(terms) > 1:
        terms = [
            terms[i] + terms[i + 1] if i + 1 < len(terms) else terms[i]
            for i in range(0, len(terms), 2)
        ]
    return terms[0]


def forecast_kernel(above, own, below, loc, state_out, picked_out, rows, columns):
    members, fields, lines, width = own.shape
    pad = rows.shape[2]
    n_rows = fields * lines * GROUP
    rows[:, :, 0:lines, :] = above[...]
    rows[:, :, lines : 2 * lines, :] = own[...]
    rows[:, :, 2 * lines : 3 * lines, :] = below[...]
    rows[:, :, 3 * lines : pad, :] = jnp.zeros((members, fields, pad - 3 * lines, width), f32)
    columns[...] = jnp.zeros(columns.shape, f32)

    def member(m, carry):
        c = [rows[m, f] for f in range(fields)]
        for _ in range(STEPS):
            n = [pltpu.roll(x, 1, 0) for x in c]
            s = [pltpu.roll(x, pad - 1, 0) for x in c]
            w = [pltpu.roll(x, 1, 1) for x in c]
            e = [pltpu.roll(x, width - 1, 1) for x in c]
            smooth = [
                (1.0 - MIX) * c[f] + MIX * 0.25 * (n[f] + s[f] + w[f] + e[f]) for f in range(fields)
            ]
            dc = [e[f] - w[f] for f in range(fields)]
            dr = [s[f] - n[f] for f in range(fields)]
            carried = [c[1] * dc[f] + c[2] * dr[f] for f in range(fields)]
            flux = (
                (1.0 + e[0]) * e[1]
                - (1.0 + w[0]) * w[1]
                + (1.0 + s[0]) * s[2]
                - (1.0 + n[0]) * n[2]
            )
            c = [
                smooth[0] - COURANT * flux,
                smooth[1] - COURANT * (carried[1] + dc[0]) + ROTATION * c[2],
                smooth[2] - COURANT * (carried[2] + dr[0]) - ROTATION * c[1],
                smooth[3] - COURANT * carried[3],
            ]
        for f in range(fields):
            mine = c[f][lines : 2 * lines]
            for t in range(width // LANES):
                at = t * n_rows + f * lines * GROUP + m
                columns[pl.ds(at, lines, stride=GROUP), :] = mine[:, t * LANES : (t + 1) * LANES]
                at = f * lines * members * GROUP + m * GROUP + t
                state_out[pl.ds(at, lines, stride=members * GROUP), :] = mine[
                    :, t * LANES : (t + 1) * LANES
                ]
        return carry

    lax.fori_loop(0, members, member, 0)

    where = loc[...]
    count = where.shape[1]
    column = where % width
    line = where // width
    onehot = (lax.broadcasted_iota(jnp.int32, (width, count), 0) == column).astype(f32).astype(bf16)
    parts = thirds(
        jnp.concatenate(
            [columns[t * n_rows : (t + 1) * n_rows, :] for t in range(width // LANES)], axis=1
        )
    )
    taken = dot_bf16(jnp.concatenate(parts, axis=0), onehot)
    taken = taken[:n_rows] + taken[n_rows : 2 * n_rows] + taken[2 * n_rows :]
    picked = tree_sum(
        jnp.where(line == d, taken[d * GROUP : (d + 1) * GROUP], 0.0)
        for d in range(fields * lines)
    )[:members]
    for r in range(picked_out.shape[0]):
        picked_out[r] = picked


def forecast(above, own, below, loc, regions):
    members, fields, lines, width = own.shape
    assert width == GROUP * LANES and members <= GROUP
    n_dest = fields * lines
    return pl.pallas_call(
        forecast_kernel,
        out_shape=[
            jax.ShapeDtypeStruct((n_dest * members * GROUP, LANES), f32),
            jax.ShapeDtypeStruct((regions, members, loc.shape[1]), f32),
        ],
        in_specs=[vmem] * 4,
        out_specs=[vmem] * 2,
        scratch_shapes=[
            pltpu.VMEM((members, fields, 4 * lines, width), f32),
            pltpu.VMEM((n_dest * GROUP * GROUP, LANES), f32),
        ],
        compiler_params=params,
        name="forecast",
    )(above, own, below, loc)


def lane_bcast(x, j):
    return jnp.broadcast_to(x[:, j : j + 1], x.shape)


def row_bcast(x, j):
    return jnp.broadcast_to(x[j : j + 1, :], x.shape)


def eliminate(m, p):
    lane = lax.broadcasted_iota(jnp.int32, (GROUP, LANES), 1)
    sub = lax.broadcasted_iota(jnp.int32, (GROUP, LANES), 0)
    base = GROUP * p
    here = (lane >= base) & (lane < base + GROUP)
    panel = m[p]
    col = [lane_bcast(panel, base + j) for j in range(GROUP)]
    panel = jnp.where(here, (lane - base == sub).astype(f32), panel)
    for j in range(GROUP):
        inv = pltpu.reciprocal(row_bcast(col[j], j))
        mine = sub == j
        row = row_bcast(panel, j) * inv
        panel = jnp.where(mine, row, panel - col[j] * row)
        for i in range(j + 1, GROUP):
            row = row_bcast(col[i], j) * inv
            col[i] = jnp.where(mine, row, col[i] - col[j] * row)
    bcast = [row_bcast(panel, j) for j in range(GROUP)]
    n = len(m)
    out = list(m)
    out[p] = panel
    for t in range(1, n):
        g = (p + t) % n
        out[g] = jnp.where(here, 0.0, m[g]) - tree_sum(
            lane_bcast(m[g], base + j) * bcast[j] for j in range(GROUP)
        )
    return out


def inverse_128(block):
    m = [block[GROUP * g : GROUP * (g + 1), :] for g in range(LANES // GROUP)]
    for p in range(LANES // GROUP):
        m = eliminate(m, p)
    return jnp.concatenate(m, axis=0)


def ring_taper(first, second, extent, inv_width):
    gap = jnp.abs(first - second)
    gap = jnp.minimum(gap, extent - gap)
    return jnp.maximum(0.0, 1.0 - gap * inv_width)


def down(row, n):
    return jnp.broadcast_to(row, (LANES, n)).T


def solve_kernel(
    inv_width, gathered, place, values, noise, variance, anom_out, weight_out, pred, cov, rhs, *, extents
):
    rows_all, cols_all = extents
    senders, blocks, per, count = gathered.shape
    members = senders * per
    tiles = count // LANES
    scale = 1.0 / (members - 1)
    for b in range(blocks):
        for s in range(senders):
            pred[b, s * per : (s + 1) * per, :] = gathered[s, b]

    def taper(b, c):
        row_b = down(place[b, 0:1, :], count)
        col_b = down(place[b, 1:2, :], count)
        row_c = place[c, 0:1, :]
        col_c = place[c, 1:2, :]
        return jnp.concatenate(
            [
                ring_taper(row_b, row_c[:, t * LANES : (t + 1) * LANES], rows_all, inv_width[b, 0])
                * ring_taper(col_b, col_c[:, t * LANES : (t + 1) * LANES], cols_all, inv_width[b, 1])
                for t in range(tiles)
            ],
            axis=1,
        )

    def block(b, carry):
        now = pred[b]
        anom = now - jnp.sum(now, axis=0, keepdims=True) * (1.0 / members)
        anom_out[b] = anom
        anom_t = anom.T
        spread = dot_exact(anom_t, anom) * scale
        diag = lax.broadcasted_iota(jnp.int32, (count, count), 0) == lax.broadcasted_iota(
            jnp.int32, (count, count), 1
        )
        cov[...] = taper(b, b) * spread + jnp.where(diag, variance[b], 0.0)
        rhs[...] = values[b] + noise[b] - now
        for k in range(tiles):
            at = slice(k * LANES, (k + 1) * LANES)
            after = slice((k + 1) * LANES, count)
            inv = inverse_128(cov[at, at])
            top = dot_exact(rhs[:, at], inv)
            rhs[:, at] = top
            if k + 1 < tiles:
                low = dot_exact(cov[after, at], inv)
                cov[after, at] = low
                across = cov[at, after]
                rhs[:, after] -= dot_exact(top, across)
                cov[after, after] -= dot_exact(low, across)
        for k in reversed(range(tiles - 1)):
            at = slice(k * LANES, (k + 1) * LANES)
            after = slice((k + 1) * LANES, count)
            rhs[:, at] -= dot_exact(rhs[:, after], cov[after, at])
        weight = rhs[...]
        weight_out[b] = weight

        def later(c, carry):
            now = pred[c]
            anom_c = now - jnp.sum(now, axis=0, keepdims=True) * (1.0 / members)
            cross = taper(b, c) * (dot_exact(anom_t, anom_c) * scale)
            pred[c] = now + dot_exact(weight, cross)
            return carry

        lax.fori_loop(b + 1, blocks, later, 0)
        return carry

    lax.fori_loop(0, blocks, block, 0)


def solve(inv_width, gathered, place, values, noise, variance, extents):
    senders, blocks, per, count = gathered.shape
    members = senders * per
    out = jax.ShapeDtypeStruct((blocks, members, count), f32)

    def body(*refs):
        solve_kernel(*refs, extents=extents)

    return pl.pallas_call(
        body,
        out_shape=[out, out],
        in_specs=[smem] + [vmem] * 5,
        out_specs=[vmem, vmem],
        scratch_shapes=[
            pltpu.VMEM((blocks, members, count), f32),
            pltpu.VMEM((count, count), f32),
            pltpu.VMEM((members, count), f32),
        ],
        compiler_params=params,
        name="solve",
    )(inv_width, gathered, place, values[:, None, :], noise, variance[:, None, :])


def update_kernel(inv_width, my_row, state, place, anom, weight, out, *, extents):
    rows_all, cols_all = extents
    blocks, members, count = anom.shape
    tiles = state.shape[0] // members
    for t in range(tiles):
        out[:, t * LANES : (t + 1) * LANES] = state[pl.ds(t, members, stride=tiles), :]
    row = my_row[0]
    for b in range(blocks):
        now = out[...]
        centered = now - jnp.sum(now, axis=0, keepdims=True) * (1.0 / members)
        cross = dot_split(anom[b].T, centered)
        obs_col = down(place[b, 1:2, :], count)
        lane = lax.broadcasted_iota(jnp.int32, (1, LANES), 1).astype(f32)
        by_row = ring_taper(row, place[b, 0:1, :], rows_all, inv_width[b, 0])
        by_col = jnp.concatenate(
            [
                ring_taper(obs_col, lane + float(t * LANES), cols_all, inv_width[b, 1])
                for t in range(tiles)
            ],
            axis=1,
        )
        out[...] = now + dot_split(weight[b] * (by_row * (1.0 / (members - 1))), by_col * cross)


def update(inv_width, my_row, state, place, anom, weight, extents):
    blocks, members, count = anom.shape
    tiles = state.shape[0] // members

    def body(*refs):
        update_kernel(*refs, extents=extents)

    return pl.pallas_call(
        body,
        out_shape=jax.ShapeDtypeStruct((members, tiles * LANES), f32),
        in_specs=[smem, smem] + [vmem] * 4,
        out_specs=vmem,
        compiler_params=params,
        name="update",
    )(inv_width, my_row, state, place, anom, weight)


def shards(
    starting_sample_set, block_owner, obs_location, taper_pairs, obs_values, obs_noise, obs_variance
):
    members, fields, lines, width = starting_sample_set.shape
    regions = lax.axis_size("reg")
    senders = lax.axis_size("mem")
    region = lax.axis_index("reg")
    mem_index = lax.axis_index("mem")
    extents = (float(lines * regions), float(width))
    assert fields * lines == senders

    forth = [(i, (i + 1) % regions) for i in range(regions)]
    back = [((i + 1) % regions, i) for i in range(regions)]
    above = lax.ppermute(starting_sample_set, "reg", forth)
    below = lax.ppermute(starting_sample_set, "reg", back)

    mine = jnp.argmax((block_owner == region).astype(jnp.int32))
    loc = lax.dynamic_slice_in_dim(obs_location, mine, 1, axis=0)
    state, picked = forecast(above, starting_sample_set, below, loc, regions)

    picked = lax.all_to_all(picked, "reg", 0, 0, tiled=True)
    picked = jnp.concatenate(
        [
            lax.dynamic_slice_in_dim(picked, block_owner[b], 1, axis=0)
            for b in range(obs_location.shape[0])
        ],
        axis=0,
    )
    gathered = lax.all_gather(picked, "mem")

    state = lax.all_to_all(
        state.reshape(senders, members * GROUP, LANES), "mem", 0, 0, tiled=True
    ).reshape(senders * members * GROUP, LANES)

    obs_row = block_owner[:, None] * lines + obs_location // width % lines
    obs_col = obs_location % width
    place = jnp.stack([obs_row, obs_col], axis=1).astype(f32)
    inv_width = 1.0 / taper_pairs.astype(f32)
    anom, weight = solve(inv_width, gathered, place, obs_values, obs_noise, obs_variance, extents)
    my_row = (region * lines + mem_index % lines).astype(f32).reshape(1)
    return update(inv_width, my_row, state, place, anom, weight, extents)


def solution(mesh):
    return jax.shard_map(
        shards,
        mesh=mesh,
        in_specs=(P("mem", None, "reg", None), P(), P(), P(), P(), P(), P()),
        out_specs=P(None, ("reg", "mem")),
        check_vma=False,
    )
```

time: 1390 us -> 163 us (0.12)
  waiting for transfers between devices: 1100 us -> 15.5 us
  other arithmetic: 137 us -> 0.75 us
  Pallas kernels: 0 us -> 79.1 us
  matrix products: 31.4 us -> 0 us
  local copies, waits for them, and re-layouts: 28.2 us -> 3.16 us
  blocking collectives: 0 us -> 19.5 us
  between operations: 21.8 us -> 7.74 us
    psum x6 -> x0, waiting for transfers between devices: 1070 us -> none  [the longest x3 731 us: spread_2(): return lax.psum(block, axis)]
    another operation x22 -> x2, other arithmetic: 120 us -> 0.72 us  [the longest x1 0.64 us: shards(): mine = jnp.argmax((block_owner == region).astype(jnp.int32))]
    pallas_call x0 -> x3, Pallas kernels: none -> 79.1 us  [the longest x1 67.8 us: solve(): pl.pallas_call(body, out_shape=[out, out], in_specs=[smem] + [vmem] * 5,...]
    dot_general x7 -> x0, matrix products: 22.5 us -> none  [the longest x3 12.2 us: assimilate(): lax.dot_general(weights, tapered, (((1,), (1,)), ((), ())), precision=hig...]
    all_gather x0 -> x1, blocking collectives: none -> 19.5 us  [shards(): gathered = lax.all_gather(picked, 'mem')]
    ppermute x8 -> x2, starting transfers between devices: 29.2 us -> 10 us  [the longest x1 6.1 us: shards(): below = lax.ppermute(starting_sample_set, 'reg', back)]
    ppermute x8 -> x2, waiting for transfers between devices: 16.6 us -> 1.07 us  [the longest x1 1.07 us: shards(): below = lax.ppermute(starting_sample_set, 'reg', back)]
  transfers between devices with their start and end apart: 15 -> 4, of which waited for: 10 -> 2; matrix products, arithmetic and copies ran while one was open for 1% -> 1% of each run, Pallas kernels for 0% -> 42%
where the time goes in v1:
time: 163 us; the launch traced here: 162 us
  Pallas kernels  79.1 us (49%)
  starting transfers between devices  36.3 us (22%)
  blocking collectives  19.5 us (12%)
  waiting for transfers between devices  15.5 us (10%)
  between operations  7.74 us (5%)
  local copies, waits for them, and re-layouts  3.16 us (2%)
    pallas_call x1, Pallas kernels, solve(): pl.pallas_call(body, out_shape=[out, out], in_specs=[smem] + [vmem] * 5,...  67.8 us
    all_gather x1, blocking collectives, shards(): gathered = lax.all_gather(picked, 'mem')  19.5 us
    all_to_all x1, starting transfers between devices, shards(): lax.all_to_all(state.reshape(senders, members * GROUP, LANES), 'mem', 0,...  14.6 us
    all_to_all x1, waiting for transfers between devices, shards(): picked = lax.all_to_all(picked, 'reg', 0, 0, tiled=True)  14.5 us
    all_to_all x1, starting transfers between devices, shards(): picked = lax.all_to_all(picked, 'reg', 0, 0, tiled=True)  11.7 us
    ppermute x1, starting transfers between devices, shards(): below = lax.ppermute(starting_sample_set, 'reg', back)  6.1 us
    pallas_call x1, Pallas kernels, forecast(): pl.pallas_call(forecast_kernel, out_shape=[jax.ShapeDtypeStruct((n_dest *...  5.79 us
    pallas_call x1, Pallas kernels, update(): pl.pallas_call(body, out_shape=jax.ShapeDtypeStruct((members, tiles * LAN...  5.54 us
  transfers between devices with their start and end apart: 4, of which 2 were waited for; matrix products, arithmetic and copies ran while one was open for 1% of the time, Pallas kernels for 42%

profile of v1, /device:TPU:1, one launch (start us, length us, event | category | flops | bytes accessed | tf_op | source)
XLA Modules:
  0.0 162.1 jit_solution(5312891888928639736)
XLA Ops:
  0.0 3.9 %collective-permute-start = (f32[5,4,4,1024]{3,2,1,0:T(4,128)}, f32[5,4,4,1024]{3,2,1,0:T(4,128)S(1)}, u32[]{:S(2)}, u32[]{:S(2)}) collective-permute-start(f32[5,4,4,1024]{3,2,1,0:T(4,128)} %own.1), channel_id=1, source_target_pairs={{0,1},{1,2},{2,3},{3,4},{4,5},{5,6},{6,7},{7,8},{8,9},{9,10},{10,1... | collective-permute-start | bytes 983048 | tf_op jit(solution)/shard_map/ppermute | solution.py:351
  3.9 6.1 %collective-permute-start.1 = (f32[5,4,4,1024]{3,2,1,0:T(4,128)}, f32[5,4,4,1024]{3,2,1,0:T(4,128)S(1)}, u32[]{:S(2)}, u32[]{:S(2)}) collective-permute-start(f32[5,4,4,1024]{3,2,1,0:T(4,128)} %own.1), channel_id=1, source_target_pairs={{1,0},{2,1},{3,2},{4,3},{5,4},{6,5},{7,6},{8,7},{9,8},{10,9},{11,1... | collective-permute-start | bytes 983048 | tf_op jit(solution)/shard_map/ppermute | solution.py:352
  10.1 0.0 copy-start.5
  10.1 0.0 copy-start.2
  10.1 0.6 copy-done.5
  10.7 0.6 fusion.4
  11.9 0.0 copy-start.6
  12.5 0.1 copy-done.6
  12.6 0.1 copy.10
  13.3 0.0 copy-done.2
  13.3 0.0 collective-permute-done.above
  13.3 1.1 collective-permute-done.1.below
  14.4 0.0 copy-start.1
  14.4 1.0 copy-done.1
  15.3 5.8 %forecast.1 = (f32[640,128]{1,0:T(8,128)}, f32[32,5,512]{2,1,0:T(8,128)}) custom-call(f32[5,4,4,1024]{3,2,1,0:T(4,128)S(1)} %collective-permute-done.above, f32[5,4,4,1024]{3,2,1,0:T(4,128)S(1)} %copy-done.1, f32[5,4,4,1024]{3,2,1,0:T(4,128)S(1)} %collective-permute-done.1.below, s32[1,512]{1,0:T(1,128)S(1)} %constant_dynamic-slice_fusion.3.loc), custom_call_target="tpu_custom_call" | custom-call | tf_op jit(solution)/shard_map/forecast/pallas_call | solution.py:135
  21.1 11.7 %all-to-all-start.1 = ((f32[32,5,512]{2,1,0:T(8,128)}), f32[32,5,512]{2,1,0:T(8,128)S(1)}, u32[]{:S(2)}, u32[]{:S(2)}) async-start(f32[32,5,512]{2,1,0:T(8,128)} %get-tuple-element.12), calls=%async_computation.1 | async-start | bytes 1048576 | tf_op jit(solution)/shard_map/all_to_all | solution.py:358
  32.8 0.1 fusion.2
  32.9 14.5 %all-to-all-done.1 = f32[32,5,512]{2,1,0:T(8,128)S(1)} async-done(((f32[32,5,512]{2,1,0:T(8,128)}), f32[32,5,512]{2,1,0:T(8,128)S(1)}, u32[]{:S(2)}, u32[]{:S(2)}) %all-to-all-start.1) | async-done | bytes 327712 | tf_op jit(solution)/shard_map/all_to_all | solution.py:358
  47.4 14.6 %all-to-all-start = ((f32[16,40,128]{2,1,0:T(8,128)}), f32[16,40,128]{2,1,0:T(8,128)S(1)}, u32[]{:S(2)}, u32[]{:S(2)}) async-start(f32[16,40,128]{2,1,0:T(8,128)} %bitcast.1), calls=%async_computation | async-start | bytes 655360 | tf_op jit(solution)/shard_map/all_to_all | solution.py:368
  61.9 0.6 fusion.5
  65.1 0.0 copy-start.3
  66.5 0.0 copy-start.4
  66.5 0.0 copy-done.3
  66.5 0.7 copy-done.4
  69.2 0.0 copy-start
  69.2 19.5 %all-gather = f32[48,5,512]{2,1,0:T(8,128)S(1)} all-gather(f32[3,5,512]{2,1,0:T(8,128)S(1)} %pad_maximum_fusion), channel_id=2, replica_groups=mesh['mem'=16,'reg'=32] {'mem'}, dimensions={0}, use_global_device_ids=true | all-gather | bytes 522240 | tf_op jit(solution)/shard_map/all_gather | solution.py:366
  88.7 0.0 copy-done
  88.7 67.8 %solve.1 = (f32[3,80,512]{2,1,0:T(8,128)S(1)}, f32[3,80,512]{2,1,0:T(8,128)S(1)}) custom-call(f32[3,2]{1,0:T(4,128)S(1)} %convert_divide_fusion.refs_0_, f32[16,3,5,512]{3,2,1,0:T(8,128)S(1)} %bitcast.9, f32[3,2,512]{2,1,0:T(2,128)S(1)} %add_convert_fusion.refs_2_.refs_3_, f32[3,1,512]{2,1,0:T(1,128)S(1)} %broadcast_in_dim.7.refs_3_, ...), custom_call_target="tpu_custom_call" | custom-call | tf_op jit(solution)/shard_map/solve/pallas_call | solution.py:282
  156.5 0.0 all-to-all-done
  156.6 5.5 %update.1 = f32[80,1024]{1,0:T(8,128)} custom-call(f32[3,2]{1,0:T(4,128)S(1)} %convert_divide_fusion.refs_0_, f32[1]{0:T(128)} %bitcast.refs_1_, f32[640,128]{1,0:T(8,128)S(1)} %bitcast.10, f32[3,2,512]{2,1,0:T(2,128)S(1)} %add_convert_fusion.refs_2_.refs_3_, f32[3,80,512]{2,1,0:T(8,128)S(1)} %get-tuple-element.13.refs_4_, ...), custom_call_target="tpu_custom_call" | custom-call | tf_op jit(solution)/shard_map/update/pallas_call | solution.py:328
  (10 shorter events, 0.1 us)
Async XLA Ops:
  0.0 13.3 %collective-permute-start = (f32[5,4,4,1024]{3,2,1,0:T(4,128)}, f32[5,4,4,1024]{3,2,1,0:T(4,128)S(1)}, u32[]{:S(2)}, u32[]{:S(2)}) collective-permute-start(f32[5,4,4,1024]{3,2,1,0:T(4,128)} %own.1), channel_id=1, source_target_pairs={{0,1},{1,2},{2,3},{3,4},{4,5},{5,6},{6,7},{7,8},{8,9},{9,10},{10,1... | collective-permute-start | bytes 983048 | tf_op jit(solution)/shard_map/ppermute | solution.py:351
  3.9 10.4 %collective-permute-start.1 = (f32[5,4,4,1024]{3,2,1,0:T(4,128)}, f32[5,4,4,1024]{3,2,1,0:T(4,128)S(1)}, u32[]{:S(2)}, u32[]{:S(2)}) collective-permute-start(f32[5,4,4,1024]{3,2,1,0:T(4,128)} %own.1), channel_id=1, source_target_pairs={{1,0},{2,1},{3,2},{4,3},{5,4},{6,5},{7,6},{8,7},{9,8},{10,9},{11,1... | collective-permute-start | bytes 983048 | tf_op jit(solution)/shard_map/ppermute | solution.py:352
  10.1 0.7 copy-start.5
  10.1 3.2 %copy-start.2 = (s32[3,512]{1,0:T(4,128)S(1)}, s32[3,512]{1,0:T(4,128)}, u32[]{:S(2)}) copy-start(s32[3,512]{1,0:T(4,128)} %param.9) | copy-start | bytes 18436
  11.9 0.7 copy-start.6
  14.4 1.0 copy-start.1
  21.1 26.2 %all-to-all-start.1 = ((f32[32,5,512]{2,1,0:T(8,128)}), f32[32,5,512]{2,1,0:T(8,128)S(1)}, u32[]{:S(2)}, u32[]{:S(2)}) async-start(f32[32,5,512]{2,1,0:T(8,128)} %get-tuple-element.12), calls=%async_computation.1 | async-start | bytes 1048576 | tf_op jit(solution)/shard_map/all_to_all | solution.py:358
  47.4 109.2 %all-to-all-start = ((f32[16,40,128]{2,1,0:T(8,128)}), f32[16,40,128]{2,1,0:T(8,128)S(1)}, u32[]{:S(2)}, u32[]{:S(2)}) async-start(f32[16,40,128]{2,1,0:T(8,128)} %bitcast.1), calls=%async_computation | async-start | bytes 655360 | tf_op jit(solution)/shard_map/all_to_all | solution.py:368
  65.1 1.4 copy-start.3
  66.5 0.7 copy-start.4
  69.2 19.5 %copy-start = (f32[3,80,512]{2,1,0:T(8,128)S(1)}, f32[3,80,512]{2,1,0:T(8,128)}, u32[]{:S(2)}) copy-start(f32[3,80,512]{2,1,0:T(8,128)} %refs_4_.1) | copy-start | bytes 1474564

commit v2 on v1

v2 whole, which is shorter than its diff:
```python
import jax
import jax.numpy as jnp
from jax import lax
from jax.experimental import pallas as pl
from jax.experimental.pallas import tpu as pltpu
from jax.sharding import PartitionSpec as P

STEPS = 4
MIX = 0.1
COURANT = 0.05
ROTATION = 0.02
LANES = 128
GROUP = 8
PANEL = 2
highest = lax.Precision.HIGHEST
f32 = jnp.float32
bf16 = jnp.bfloat16

vmem = pl.BlockSpec(memory_space=pltpu.VMEM)
smem = pl.BlockSpec(memory_space=pltpu.SMEM)
params = pltpu.CompilerParams(vmem_limit_bytes=48 * 1024 * 1024)


def dot_exact(a, b):
    return lax.dot_general(
        a, b, (((1,), (0,)), ((), ())), precision=highest, preferred_element_type=f32
    )


def dot_bf16(a, b):
    return lax.dot_general(a, b, (((1,), (0,)), ((), ())), preferred_element_type=f32)


def halves(x):
    hi = x.astype(bf16)
    return hi, (x - hi.astype(f32)).astype(bf16)


def thirds(x):
    hi = x.astype(bf16)
    rest = x - hi.astype(f32)
    mid = rest.astype(bf16)
    return hi, mid, (rest - mid.astype(f32)).astype(bf16)


def dot_split(a, b):
    a_hi, a_lo = halves(a)
    b_hi, b_lo = halves(b)
    return dot_bf16(
        jnp.concatenate([a_hi, a_hi, a_lo], axis=1), jnp.concatenate([b_hi, b_lo, b_hi], axis=0)
    )


def stacked(x):
    hi = x.astype(bf16).astype(f32)
    lo = x - hi
    return jnp.concatenate([hi, hi, lo], axis=0)


def dot_stacked(left, b):
    b_hi, b_lo = halves(b)
    return dot_bf16(left, jnp.concatenate([b_hi, b_lo, b_hi], axis=0))


def tree_sum(terms):
    terms = list(terms)
    while len(terms) > 1:
        terms = [
            terms[i] + terms[i + 1] if i + 1 < len(terms) else terms[i]
            for i in range(0, len(terms), 2)
        ]
    return terms[0]


def forecast_kernel(
    above, own, below, loc, state_out, picked_out, rows, columns, *, picked_rows
):
    members, fields, lines, width = own.shape
    pad = rows.shape[2]
    n_rows = fields * lines * GROUP
    rows[:, :, 0:lines, :] = above[...]
    rows[:, :, lines : 2 * lines, :] = own[...]
    rows[:, :, 2 * lines : 3 * lines, :] = below[...]
    rows[:, :, 3 * lines : pad, :] = jnp.zeros((members, fields, pad - 3 * lines, width), f32)
    columns[...] = jnp.zeros(columns.shape, f32)

    def member(m, carry):
        c = [rows[m, f] for f in range(fields)]
        for _ in range(STEPS):
            n = [pltpu.roll(x, 1, 0) for x in c]
            s = [pltpu.roll(x, pad - 1, 0) for x in c]
            w = [pltpu.roll(x, 1, 1) for x in c]
            e = [pltpu.roll(x, width - 1, 1) for x in c]
            smooth = [
                (1.0 - MIX) * c[f] + MIX * 0.25 * (n[f] + s[f] + w[f] + e[f]) for f in range(fields)
            ]
            dc = [e[f] - w[f] for f in range(fields)]
            dr = [s[f] - n[f] for f in range(fields)]
            carried = [c[1] * dc[f] + c[2] * dr[f] for f in range(fields)]
            flux = (
                (1.0 + e[0]) * e[1]
                - (1.0 + w[0]) * w[1]
                + (1.0 + s[0]) * s[2]
                - (1.0 + n[0]) * n[2]
            )
            c = [
                smooth[0] - COURANT * flux,
                smooth[1] - COURANT * (carried[1] + dc[0]) + ROTATION * c[2],
                smooth[2] - COURANT * (carried[2] + dr[0]) - ROTATION * c[1],
                smooth[3] - COURANT * carried[3],
            ]
        for f in range(fields):
            mine = c[f][lines : 2 * lines]
            for t in range(width // LANES):
                at = t * n_rows + f * lines * GROUP + m
                columns[pl.ds(at, lines, stride=GROUP), :] = mine[:, t * LANES : (t + 1) * LANES]
                at = f * lines * members * GROUP + m * GROUP + t
                state_out[pl.ds(at, lines, stride=members * GROUP), :] = mine[
                    :, t * LANES : (t + 1) * LANES
                ]
        return carry

    lax.fori_loop(0, members, member, 0)

    where = loc[...]
    count = where.shape[1]
    column = where % width
    line = where // width
    onehot = (lax.broadcasted_iota(jnp.int32, (width, count), 0) == column).astype(f32).astype(bf16)
    parts = thirds(
        jnp.concatenate(
            [columns[t * n_rows : (t + 1) * n_rows, :] for t in range(width // LANES)], axis=1
        )
    )
    taken = dot_bf16(jnp.concatenate(parts, axis=0), onehot)
    taken = taken[:n_rows] + taken[n_rows : 2 * n_rows] + taken[2 * n_rows :]
    picked = tree_sum(
        jnp.where(line == d, taken[d * GROUP : (d + 1) * GROUP], 0.0)
        for d in range(fields * lines)
    )[:members]
    chunks = count // LANES
    for r in range(picked_out.shape[0] // picked_rows):
        for t in range(chunks):
            picked_out[pl.ds(r * picked_rows + t, members, stride=chunks), :] = picked[
                :, t * LANES : (t + 1) * LANES
            ]


def forecast(above, own, below, loc, regions):
    members, fields, lines, width = own.shape
    assert width == GROUP * LANES and members <= GROUP
    n_dest = fields * lines
    picked_rows = -(-members * loc.shape[1] // (LANES * GROUP)) * GROUP

    def body(*refs):
        forecast_kernel(*refs, picked_rows=picked_rows)

    return pl.pallas_call(
        body,
        out_shape=[
            jax.ShapeDtypeStruct((n_dest * members * GROUP, LANES), f32),
            jax.ShapeDtypeStruct((regions * picked_rows, LANES), f32),
        ],
        in_specs=[vmem] * 4,
        out_specs=[vmem] * 2,
        scratch_shapes=[
            pltpu.VMEM((members, fields, 4 * lines, width), f32),
            pltpu.VMEM((n_dest * GROUP * GROUP, LANES), f32),
        ],
        compiler_params=params,
        name="forecast",
    )(above, own, below, loc)


def lane_bcast(x, j):
    return jnp.broadcast_to(x[:, j : j + 1], x.shape)


def row_bcast(x, j):
    return jnp.broadcast_to(x[j : j + 1, :], x.shape)


def eliminate(m, p, zeros):
    width = PANEL * GROUP
    lane = lax.broadcasted_iota(jnp.int32, (GROUP, LANES), 1)
    sub = lax.broadcasted_iota(jnp.int32, (GROUP, LANES), 0)
    base = width * p
    here = (lane >= base) & (lane < base + width)
    own = range(PANEL * p, PANEL * (p + 1))
    col = [[lane_bcast(m[g], base + j) + zeros for g in own] for j in range(width)]
    col.append(
        [
            jnp.where(here, (lane - base == sub + GROUP * i).astype(f32), m[g])
            for i, g in enumerate(own)
        ]
    )
    for j in range(width):
        mine, at = divmod(j, GROUP)
        inv = pltpu.reciprocal(row_bcast(col[j][mine], at))
        pivot = sub == at
        coef = list(col[j])
        coef[mine] = jnp.where(pivot, -1.0, coef[mine])
        for k in range(j + 1, width + 1):
            row = row_bcast(col[k][mine], at)
            old = list(col[k])
            old[mine] = jnp.where(pivot, 0.0, old[mine])
            if k == j + 1:
                col[k] = [old[g] - (coef[g] * row) * inv for g in range(PANEL)]
            else:
                row = row * inv
                col[k] = [old[g] - coef[g] * row for g in range(PANEL)]
    panel = col[width]
    out = list(m)
    for i, g in enumerate(own):
        out[g] = panel[i]
    n = len(m)
    after = range(PANEL * (p + 1), min(n, PANEL * (p + 2)))
    rows = [row_bcast(panel[j // GROUP], j % GROUP) for j in range(width)]
    for g in after:
        out[g] = jnp.where(here, 0.0, m[g]) - tree_sum(
            lane_bcast(m[g], base + j) * rows[j] for j in range(width)
        )
    rest = [g for g in range(n) if g not in own and g not in after]
    right = [jnp.zeros((base, LANES), f32)] if base else []
    right += panel
    if base + width < LANES:
        right.append(jnp.zeros((LANES - base - width, LANES), f32))
    change = dot_exact(
        jnp.concatenate([m[g] for g in rest], axis=0), jnp.concatenate(right, axis=0)
    )
    for t, g in enumerate(rest):
        out[g] = jnp.where(here, 0.0, m[g]) - change[GROUP * t : GROUP * (t + 1)]
    return out


def inverse_128(block, zeros):
    m = [block[GROUP * g : GROUP * (g + 1), :] for g in range(LANES // GROUP)]
    for p in range(LANES // (GROUP * PANEL)):
        m = eliminate(m, p, zeros)
    return jnp.concatenate(m, axis=0)


def ring_taper(first, second, extent, inv_width):
    gap = jnp.abs(first - second)
    gap = jnp.minimum(gap, extent - gap)
    return jnp.maximum(0.0, 1.0 - gap * inv_width)


def down(row, n):
    return jnp.broadcast_to(row, (LANES, n)).T


def obs_place(owner, location, width, lines):
    row = owner * lines + (location // width) % lines
    return row.astype(f32), (location % width).astype(f32)


def inverse_of(scalar):
    return pltpu.reciprocal(jnp.full((1, LANES), scalar.astype(f32), f32))


def across(row, fn):
    return jnp.concatenate(
        [fn(row[:, t : t + LANES]) for t in range(0, row.shape[1], LANES)], axis=1
    )


def solve_kernel(
    owner, widths, gathered, location, values, noise, variance, zero,
    anom_out, weight_out, pred, cov, rhs, *, extents, lines, picked_rows
):
    blocks, members, count = noise.shape
    rows_all, cols_all = extents
    tiles = count // LANES
    scale = 1.0 / (members - 1)
    senders = gathered.shape[0] // (blocks * picked_rows)
    per = members // senders
    zeros = zero[...]
    for b in range(blocks):
        for s in range(senders):
            for t in range(tiles):
                pred[b, s * per : (s + 1) * per, t * LANES : (t + 1) * LANES] = gathered[
                    pl.ds((s * blocks + b) * picked_rows + t, per, stride=tiles), :
                ]

    def taper(b, c):
        row_b, col_b = obs_place(owner[b], location[pl.ds(b, 1), :], cols_all, lines)
        row_c, col_c = obs_place(owner[c], location[pl.ds(c, 1), :], cols_all, lines)
        row_b, col_b = down(row_b, count), down(col_b, count)
        inv_row, inv_col = inverse_of(widths[b, 0]), inverse_of(widths[b, 1])
        return across(row_c, lambda x: ring_taper(row_b, x, float(rows_all), inv_row)) * across(
            col_c, lambda x: ring_taper(col_b, x, float(cols_all), inv_col)
        )

    def block(b, carry):
        now = pred[b]
        anom = now - jnp.sum(now, axis=0, keepdims=True) * (1.0 / members)
        anom_out[b] = anom
        spread = dot_exact(anom.T, anom) * scale
        diag = lax.broadcasted_iota(jnp.int32, (count, count), 0) == lax.broadcasted_iota(
            jnp.int32, (count, count), 1
        )
        cov[...] = taper(b, b) * spread + jnp.where(diag, variance[pl.ds(b, 1), :], 0.0)
        rhs[...] = values[pl.ds(b, 1), :] + noise[b] - now
        corner = cov[0:LANES, 0:LANES]
        for k in range(tiles):
            at = slice(k * LANES, (k + 1) * LANES)
            inv = inverse_128(corner, zeros)
            if k + 1 < tiles:
                after = slice((k + 1) * LANES, count)
                soon = slice((k + 1) * LANES, (k + 2) * LANES)
                low_soon = dot_exact(cov[soon, at], inv)
                corner = cov[soon, soon] - dot_exact(low_soon, cov[at, soon])
                if k + 2 < tiles:
                    late = slice((k + 2) * LANES, count)
                    low_late = dot_exact(cov[late, at], inv)
                    cov[soon, late] -= dot_exact(low_soon, cov[at, late])
                    cov[late, after] -= dot_exact(low_late, cov[at, after])
                    cov[late, at] = low_late
                top = dot_exact(rhs[:, at], inv)
                rhs[:, at] = top
                rhs[:, after] -= dot_exact(top, cov[at, after])
                cov[soon, at] = low_soon
            else:
                rhs[:, at] = dot_exact(rhs[:, at], inv)
        for k in reversed(range(tiles - 1)):
            at = slice(k * LANES, (k + 1) * LANES)
            after = slice((k + 1) * LANES, count)
            rhs[:, at] -= dot_exact(rhs[:, after], cov[after, at])
        weight = rhs[...]
        weight_out[b] = weight

        def later(c, carry):
            now = pred[c]
            anom_c = now - jnp.sum(now, axis=0, keepdims=True) * (1.0 / members)
            left = stacked(anom_out[b]).T.astype(bf16)
            cross = taper(b, c) * (dot_stacked(left, anom_c) * scale)
            pred[c] = now + dot_split(weight_out[b], cross)
            return carry

        lax.fori_loop(b + 1, blocks, later, 0)
        return carry

    lax.fori_loop(0, blocks, block, 0)


def solve(owner, widths, gathered, location, values, noise, variance, extents, lines, picked_rows):
    blocks, members, count = noise.shape
    out = jax.ShapeDtypeStruct((blocks, members, count), f32)

    def body(*refs):
        solve_kernel(*refs, extents=extents, lines=lines, picked_rows=picked_rows)

    return pl.pallas_call(
        body,
        out_shape=[out, out],
        in_specs=[smem, smem] + [vmem] * 6,
        out_specs=[vmem, vmem],
        scratch_shapes=[
            pltpu.VMEM((blocks, members, count), f32),
            pltpu.VMEM((count, count), f32),
            pltpu.VMEM((members, count), f32),
        ],
        compiler_params=params,
        name="solve",
    )(owner, widths, gathered, location, values, noise, variance, jnp.zeros((GROUP, LANES), f32))


def update_kernel(owner, widths, my_row, state, location, anom, weight, out, *, extents, lines):
    rows_all, cols_all = extents
    blocks, members, count = anom.shape
    tiles = state.shape[0] // members
    for t in range(tiles):
        out[:, t * LANES : (t + 1) * LANES] = state[pl.ds(t, members, stride=tiles), :]
    row = my_row[0].astype(f32)
    for b in range(blocks):
        now = out[...]
        centered = now - jnp.sum(now, axis=0, keepdims=True) * (1.0 / members)
        cross = dot_stacked(stacked(anom[b]).T.astype(bf16), centered)
        obs_row, obs_col = obs_place(owner[b], location[b : b + 1, :], cols_all, lines)
        obs_col = down(obs_col, count)
        lane = lax.broadcasted_iota(jnp.int32, (1, tiles * LANES), 1).astype(f32)
        inv_row, inv_col = inverse_of(widths[b, 0]), inverse_of(widths[b, 1])
        by_row = across(obs_row, lambda x: ring_taper(row, x, float(rows_all), inv_row))
        by_col = across(lane, lambda x: ring_taper(obs_col, x, float(cols_all), inv_col))
        out[...] = now + dot_split(weight[b] * (by_row * (1.0 / (members - 1))), by_col * cross)


def update(owner, widths, my_row, state, location, anom, weight, extents, lines):
    blocks, members, count = anom.shape
    tiles = state.shape[0] // members

    def body(*refs):
        update_kernel(*refs, extents=extents, lines=lines)

    return pl.pallas_call(
        body,
        out_shape=jax.ShapeDtypeStruct((members, tiles * LANES), f32),
        in_specs=[smem] * 3 + [vmem] * 4,
        out_specs=vmem,
        compiler_params=params,
        name="update",
    )(owner, widths, my_row, state, location, anom, weight)


def choose_kernel(owner, received, out):
    for b in range(out.shape[0]):
        out[b] = received[owner[b]]


def choose(owner, received):
    return pl.pallas_call(
        choose_kernel,
        out_shape=jax.ShapeDtypeStruct(owner.shape + received.shape[1:], f32),
        in_specs=[smem, vmem],
        out_specs=vmem,
        compiler_params=params,
        name="choose",
    )(owner, received)


def shards(
    starting_sample_set, block_owner, obs_location, taper_pairs, obs_values, obs_noise, obs_variance
):
    members, fields, lines, width = starting_sample_set.shape
    regions = lax.axis_size("reg")
    senders = lax.axis_size("mem")
    region = lax.axis_index("reg")
    mem_index = lax.axis_index("mem")
    extents = (lines * regions, width)
    assert fields * lines == senders

    forth = [(i, (i + 1) % regions) for i in range(regions)]
    back = [((i + 1) % regions, i) for i in range(regions)]
    above = lax.ppermute(starting_sample_set, "reg", forth)
    below = lax.ppermute(starting_sample_set, "reg", back)

    mine = jnp.argmax((block_owner == region).astype(jnp.int32))
    loc = lax.dynamic_slice_in_dim(obs_location, mine, 1, axis=0)
    state, picked = forecast(above, starting_sample_set, below, loc, regions)

    picked_rows = picked.shape[0] // regions
    picked = lax.all_to_all(
        picked.reshape(regions, picked_rows, LANES), "reg", 0, 0, tiled=True
    )
    gathered = lax.all_gather(choose(block_owner, picked), "mem").reshape(-1, LANES)

    state = lax.all_to_all(
        state.reshape(senders, members * GROUP, LANES), "mem", 0, 0, tiled=True
    ).reshape(senders * members * GROUP, LANES)

    anom, weight = solve(
        block_owner, taper_pairs, gathered, obs_location, obs_values, obs_noise, obs_variance,
        extents, lines, picked_rows,
    )
    my_row = (region * lines + mem_index % lines).reshape(1)
    return update(
        block_owner, taper_pairs, my_row, state, obs_location, anom, weight, extents, lines
    )


def solution(mesh):
    return jax.shard_map(
        shards,
        mesh=mesh,
        in_specs=(P("mem", None, "reg", None), P(), P(), P(), P(), P(), P()),
        out_specs=P(None, ("reg", "mem")),
        check_vma=False,
    )
```

time: 163 us -> 133 us (0.82)
  blocking collectives: 19.5 us -> 44.7 us
  Pallas kernels: 79.1 us -> 56.6 us
  waiting for transfers between devices: 15.5 us -> 1.01 us
  starting transfers between devices: 36.3 us -> 24.9 us
  between operations: 7.74 us -> 2 us
    all_to_all x0 -> x1, blocking collectives: none -> 23.3 us  [shards(): lax.all_to_all(picked.reshape(regions, picked_rows, LANES), 'reg', 0, 0,...]
    pallas_call x2 -> x3, Pallas kernels: 73.6 us -> 51.5 us  [the longest x1 45.8 us: solve(): pl.pallas_call(body, out_shape=[out, out], in_specs=[smem, smem] + [vmem]...]
    all_to_all x1 -> x0, waiting for transfers between devices: 14.5 us -> none  [shards(): picked = lax.all_to_all(picked, 'reg', 0, 0, tiled=True)]
    all_to_all x1 -> x0, starting transfers between devices: 11.7 us -> none  [shards(): picked = lax.all_to_all(picked, 'reg', 0, 0, tiled=True)]
    all_gather x1, blocking collectives: 19.5 us -> 21.4 us  [shards(): lax.all_gather(choose(block_owner, picked), 'mem').reshape(-1, LANES)]
  transfers between devices with their start and end apart: 4 -> 3, of which waited for: 2 -> 1; matrix products, arithmetic and copies ran while one was open for 1% -> 1% of each run, Pallas kernels for 42% -> 35%
where the time goes in v2:
time: 133 us
  Pallas kernels  56.6 us (43%)
  blocking collectives  44.7 us (34%)
  starting transfers between devices  24.9 us (19%)
  local copies, waits for them, and re-layouts  2.42 us (2%)
  between operations  2 us (2%)
  other arithmetic  1.37 us (1%)
    pallas_call x1, Pallas kernels, solve(): pl.pallas_call(body, out_shape=[out, out], in_specs=[smem, smem] + [vmem]...  45.8 us
    all_to_all x1, blocking collectives, shards(): lax.all_to_all(picked.reshape(regions, picked_rows, LANES), 'reg', 0, 0,...  23.3 us
    all_gather x1, blocking collectives, shards(): lax.all_gather(choose(block_owner, picked), 'mem').reshape(-1, LANES)  21.4 us
    all_to_all x1, starting transfers between devices, shards(): lax.all_to_all(state.reshape(senders, members * GROUP, LANES), 'mem', 0,...  14.7 us
    ppermute x1, starting transfers between devices, shards(): below = lax.ppermute(starting_sample_set, 'reg', back)  6.1 us
    pallas_call x1, Pallas kernels, update(): pl.pallas_call(body, out_shape=jax.ShapeDtypeStruct((members, tiles * LAN...  5.17 us
    pallas_call x1, Pallas kernels, forecast(): pl.pallas_call(body, out_shape=[jax.ShapeDtypeStruct((n_dest * members *...  5.09 us
    ppermute x1, starting transfers between devices, shards(): above = lax.ppermute(starting_sample_set, 'reg', forth)  4.07 us
  transfers between devices with their start and end apart: 3, of which 1 were waited for; matrix products, arithmetic and copies ran while one was open for 1% of the time, Pallas kernels for 35%

profile of v2, /device:TPU:1, one launch (start us, length us, event | category | flops | bytes accessed | tf_op | source)
XLA Modules:
  0.0 133.0 jit_solution(10022143880762176086)
XLA Ops:
  0.0 0.0 copy-start.2
  0.0 4.1 %collective-permute-start = (f32[5,4,4,1024]{3,2,1,0:T(4,128)}, f32[5,4,4,1024]{3,2,1,0:T(4,128)S(1)}, u32[]{:S(2)}, u32[]{:S(2)}) collective-permute-start(f32[5,4,4,1024]{3,2,1,0:T(4,128)} %refs_1_.3), channel_id=1, source_target_pairs={{0,1},{1,2},{2,3},{3,4},{4,5},{5,6},{6,7},{7,8},{8,9},{9,10},{10,1... | collective-permute-start | bytes 983048 | tf_op jit(solution)/shard_map/ppermute | solution.py:435
  4.1 6.1 %collective-permute-start.1 = (f32[5,4,4,1024]{3,2,1,0:T(4,128)}, f32[5,4,4,1024]{3,2,1,0:T(4,128)S(1)}, u32[]{:S(2)}, u32[]{:S(2)}) collective-permute-start(f32[5,4,4,1024]{3,2,1,0:T(4,128)} %refs_1_.3), channel_id=1, source_target_pairs={{1,0},{2,1},{3,2},{4,3},{5,4},{6,5},{7,6},{8,7},{9,8},{10,9},{11,1... | collective-permute-start | bytes 983048 | tf_op jit(solution)/shard_map/ppermute | solution.py:436
  10.2 1.4 %fusion = (s32[]{:T(128)}, s32[]{:T(128)}) fusion(s32[3]{0:T(128)} %refs_0_.3, s32[]{:T(128)S(6)} %axis_index.22), kind=kLoop, calls=%fused_computation.1 | loop fusion | flops 20 | bytes 24 | tf_op jit(solution)/shard_map/shards/reduce | solution.py:438
  13.5 0.0 copy-done.2
  13.5 0.0 collective-permute-done.refs_0_
  13.5 1.0 collective-permute-done.1.refs_2_
  14.5 0.0 copy-start.1
  14.5 1.0 copy-done.1
  15.5 5.1 %forecast.1 = (f32[640,128]{1,0:T(8,128)}, f32[768,128]{1,0:T(8,128)S(1)}) custom-call(f32[5,4,4,1024]{3,2,1,0:T(4,128)S(1)} %collective-permute-done.refs_0_, f32[5,4,4,1024]{3,2,1,0:T(4,128)S(1)} %copy-done.1, f32[5,4,4,1024]{3,2,1,0:T(4,128)S(1)} %collective-permute-done.1.refs_2_, s32[1,512]{1,0:T(1,128)S(1)} %constant_dynamic-slice_fusion.refs_3_), custom_call_target="tpu_custom_call" | custom-call | tf_op jit(solution)/shard_map/forecast/pallas_call | solution.py:158
  20.6 23.3 %all_to_all.10.received = f32[32,24,128]{2,1,0:T(8,128)S(1)} all-to-all(f32[32,24,128]{2,1,0:T(8,128)S(1)} %bitcast.7), channel_id=1, replica_groups=mesh['mem'=16,'reg'=32] {'reg'}, dimensions={0} | all-to-all | bytes 786432 | tf_op jit(solution)/shard_map/all_to_all | solution.py:443
  43.8 14.7 %all-to-all-start = ((f32[16,40,128]{2,1,0:T(8,128)}), f32[16,40,128]{2,1,0:T(8,128)S(1)}, u32[]{:S(2)}, u32[]{:S(2)}) async-start(f32[16,40,128]{2,1,0:T(8,128)} %bitcast.1), calls=%async_computation | async-start | bytes 655360 | tf_op jit(solution)/shard_map/all_to_all | solution.py:448
  58.6 0.0 copy-start.6
  58.6 0.7 copy-done.6
  59.2 0.1 copy.11.refs_1_
  59.3 0.0 copy-start.5
  59.3 0.7 copy-done.5
  60.0 0.0 copy-start
  60.0 0.5 choose.1
  60.6 0.0 copy-start.3
  60.6 0.0 copy-start.4
  60.6 21.4 %all-gather = f32[48,24,128]{2,1,0:T(8,128)S(1)} all-gather(f32[3,24,128]{2,1,0:T(8,128)S(1)} %choose.1), channel_id=2, replica_groups=mesh['mem'=16,'reg'=32] {'mem'}, dimensions={0}, use_global_device_ids=true | all-gather | bytes 626688 | tf_op jit(solution)/shard_map/all_gather | solution.py:446
  82.0 0.0 copy-done
  82.0 0.0 copy-done.3
  82.0 0.0 copy-done.4
  82.0 45.8 %solve.1 = (f32[3,80,512]{2,1,0:T(8,128)S(1)}, f32[3,80,512]{2,1,0:T(8,128)S(1)}) custom-call(s32[3]{0:T(128)S(1)} %copy-done.5, s32[3,2]{1,0:T(4,128)S(1)} %copy.11.refs_1_, f32[1152,128]{1,0:T(8,128)S(1)} %bitcast.5, s32[3,512]{1,0:T(4,128)S(1)} %copy-done.2, f32[3,512]{1,0:T(4,128)S(1)} %copy-done.3, f32[3,80,512]{2,1,0:T(8,128)S(1)} %copy-done, ...), custom_call_target="tpu_custom_call" | custom-call | tf_op jit(solution)/shard_map/solve/pallas_call | solution.py:354
  127.9 0.0 all-to-all-done
  127.9 5.2 %update.1 = f32[80,1024]{1,0:T(8,128)} custom-call(s32[3]{0:T(128)S(1)} %copy-done.5, s32[3,2]{1,0:T(4,128)S(1)} %copy.11.refs_1_, s32[1]{0:T(128)} %bitcast.refs_2_, f32[640,128]{1,0:T(8,128)S(1)} %bitcast.6, s32[3,512]{1,0:T(4,128)S(1)} %copy-done.2, f32[3,80,512]{2,1,0:T(8,128)S(1)} %get-tuple-element.13.refs_5_, f32[3,80,512]{2,1,0:T(8,128)S(1)} %get-tuple-element.14.refs_6_), custom_call_target="tpu_custom_call" | custom-call | tf_op jit(solution)/shard_map/update/pallas_call | solution.py:396
  (2 shorter events, 0.0 us)
Async XLA Ops:
  0.0 13.5 %copy-start.2 = (s32[3,512]{1,0:T(4,128)S(1)}, s32[3,512]{1,0:T(4,128)}, u32[]{:S(2)}) copy-start(s32[3,512]{1,0:T(4,128)} %refs_4_.3) | copy-start | bytes 18436
  0.0 13.5 %collective-permute-start = (f32[5,4,4,1024]{3,2,1,0:T(4,128)}, f32[5,4,4,1024]{3,2,1,0:T(4,128)S(1)}, u32[]{:S(2)}, u32[]{:S(2)}) collective-permute-start(f32[5,4,4,1024]{3,2,1,0:T(4,128)} %refs_1_.3), channel_id=1, source_target_pairs={{0,1},{1,2},{2,3},{3,4},{4,5},{5,6},{6,7},{7,8},{8,9},{9,10},{10,1... | collective-permute-start | bytes 983048 | tf_op jit(solution)/shard_map/ppermute | solution.py:435
  4.1 10.4 %collective-permute-start.1 = (f32[5,4,4,1024]{3,2,1,0:T(4,128)}, f32[5,4,4,1024]{3,2,1,0:T(4,128)S(1)}, u32[]{:S(2)}, u32[]{:S(2)}) collective-permute-start(f32[5,4,4,1024]{3,2,1,0:T(4,128)} %refs_1_.3), channel_id=1, source_target_pairs={{1,0},{2,1},{3,2},{4,3},{5,4},{6,5},{7,6},{8,7},{9,8},{10,9},{11,1... | collective-permute-start | bytes 983048 | tf_op jit(solution)/shard_map/ppermute | solution.py:436
  14.5 1.0 copy-start.1
  43.8 84.0 %all-to-all-start = ((f32[16,40,128]{2,1,0:T(8,128)}), f32[16,40,128]{2,1,0:T(8,128)S(1)}, u32[]{:S(2)}, u32[]{:S(2)}) async-start(f32[16,40,128]{2,1,0:T(8,128)} %bitcast.1), calls=%async_computation | async-start | bytes 655360 | tf_op jit(solution)/shard_map/all_to_all | solution.py:448
  58.6 0.7 copy-start.6
  59.3 0.7 copy-start.5
  60.0 22.0 %copy-start = (f32[3,80,512]{2,1,0:T(8,128)S(1)}, f32[3,80,512]{2,1,0:T(8,128)}, u32[]{:S(2)}) copy-start(f32[3,80,512]{2,1,0:T(8,128)} %refs_5_.1) | copy-start | bytes 1474564
  60.6 21.4 %copy-start.3 = (f32[3,512]{1,0:T(4,128)S(1)}, f32[3,512]{1,0:T(4,128)}, u32[]{:S(2)}) copy-start(f32[3,512]{1,0:T(4,128)} %refs_4_.2) | copy-start | bytes 18436
  60.6 21.4 %copy-start.4 = (f32[3,512]{1,0:T(4,128)S(1)}, f32[3,512]{1,0:T(4,128)}, u32[]{:S(2)}) copy-start(f32[3,512]{1,0:T(4,128)} %refs_6_.1) | copy-start | bytes 18436

commit v3 on v2

--- a/solution.py
+++ b/solution.py
@@ -18,7 +18,7 @@
 
 vmem = pl.BlockSpec(memory_space=pltpu.VMEM)
 smem = pl.BlockSpec(memory_space=pltpu.SMEM)
-params = pltpu.CompilerParams(vmem_limit_bytes=48 * 1024 * 1024)
+params = pltpu.CompilerParams(vmem_limit_bytes=32 * 1024 * 1024)
 
 
 def dot_exact(a, b):
@@ -265,137 +265,196 @@
     )
 
 
-def solve_kernel(
+def prepare_kernel(owner, region, location, own, loc, own_copy):
+    own_copy[...] = own[...]
+    mine = location[0:1, :]
+    for b in range(1, location.shape[0]):
+        mine = jnp.where(owner[b] == region[0], location[b : b + 1, :], mine)
+    loc[...] = mine
+
+
+def prepare(owner, region, location, own):
+    return pl.pallas_call(
+        prepare_kernel,
+        out_shape=[
+            jax.ShapeDtypeStruct((1, location.shape[1]), jnp.int32),
+            jax.ShapeDtypeStruct(own.shape, f32),
+        ],
+        in_specs=[smem] * 2 + [vmem] * 2,
+        out_specs=[vmem] * 2,
+        compiler_params=params,
+        name="prepare",
+    )(owner, region, location, own)
+
+
+def obs_taper(owner, widths, location, b, c, extents, lines):
+    rows_all, cols_all = extents
+    row_b, col_b = obs_place(owner[b], location[pl.ds(b, 1), :], cols_all, lines)
+    row_c, col_c = obs_place(owner[c], location[pl.ds(c, 1), :], cols_all, lines)
+    row_b, col_b = down(row_b, row_b.shape[1]), down(col_b, col_b.shape[1])
+    inv_row, inv_col = inverse_of(widths[b, 0]), inverse_of(widths[b, 1])
+    return across(row_c, lambda x: ring_taper(row_b, x, float(rows_all), inv_row)) * across(
+        col_c, lambda x: ring_taper(col_b, x, float(cols_all), inv_col)
+    )
+
+
+def anomaly(x):
+    return x - jnp.sum(x, axis=0, keepdims=True) * (1.0 / x.shape[0])
+
+
+def unpack(gathered, first, senders, stride, per, tiles, out, b):
+    for s in range(senders):
+        for t in range(tiles):
+            out[b, s * per : (s + 1) * per, t * LANES : (t + 1) * LANES] = gathered[
+                pl.ds(s * stride + first + t, per, stride=tiles), :
+            ]
+
+
+def weights_of(now, taper, misfit, variance, zeros, cov, rhs):
+    members, count = now.shape
+    tiles = count // LANES
+    anom = anomaly(now)
+    spread = dot_exact(anom.T, anom) * (1.0 / (members - 1))
+    diag = lax.broadcasted_iota(jnp.int32, (count, count), 0) == lax.broadcasted_iota(
+        jnp.int32, (count, count), 1
+    )
+    cov[...] = taper * spread + jnp.where(diag, variance, 0.0)
+    rhs[...] = misfit
+    corner = cov[0:LANES, 0:LANES]
+    for k in range(tiles):
+        at = slice(k * LANES, (k + 1) * LANES)
+        inv = inverse_128(corner, zeros)
+        if k + 1 < tiles:
+            after = slice((k + 1) * LANES, count)
+            soon = slice((k + 1) * LANES, (k + 2) * LANES)
+            low_soon = dot_exact(cov[soon, at], inv)
+            corner = cov[soon, soon] - dot_exact(low_soon, cov[at, soon])
+            if k + 2 < tiles:
+                late = slice((k + 2) * LANES, count)
+                low_late = dot_exact(cov[late, at], inv)
+                cov[soon, late] -= dot_exact(low_soon, cov[at, late])
+                cov[late, after] -= dot_exact(low_late, cov[at, after])
+                cov[late, at] = low_late
+            top = dot_exact(rhs[:, at], inv)
+            rhs[:, at] = top
+            rhs[:, after] -= dot_exact(top, cov[at, after])
+            cov[soon, at] = low_soon
+        else:
+            rhs[:, at] = dot_exact(rhs[:, at], inv)
+    for k in reversed(range(tiles - 1)):
+        at = slice(k * LANES, (k + 1) * LANES)
+        after = slice((k + 1) * LANES, count)
+        rhs[:, at] -= dot_exact(rhs[:, after], cov[after, at])
+    return anom, rhs[...]
+
+
+def first_kernel(
     owner, widths, gathered, location, values, noise, variance, zero,
-    anom_out, weight_out, pred, cov, rhs, *, extents, lines, picked_rows
+    anom_out, weight_out, pred, cov, rhs, *, senders, extents, lines
+):
+    members, count = anom_out.shape
+    taper = obs_taper(owner, widths, location, 0, 0, extents, lines)
+    unpack(gathered, 0, senders, gathered.shape[0] // senders, members // senders, count // LANES, pred, 0)
+    now = pred[0]
+    anom_out[...], weight_out[...] = weights_of(
+        now, taper, values[0:1, :] + noise[0] - now, variance[0:1, :], zero[...], cov, rhs
+    )
+
+
+def rest_kernel(
+    owner, widths, gathered, location, values, noise, variance, zero, anom_first, weight_first,
+    anom_out, weight_out, pred, cov, rhs, *, senders, extents, lines, skip, picked_rows
 ):
     blocks, members, count = noise.shape
-    rows_all, cols_all = extents
     tiles = count // LANES
-    scale = 1.0 / (members - 1)
-    senders = gathered.shape[0] // (blocks * picked_rows)
-    per = members // senders
-    zeros = zero[...]
-    for b in range(blocks):
-        for s in range(senders):
-            for t in range(tiles):
-                pred[b, s * per : (s + 1) * per, t * LANES : (t + 1) * LANES] = gathered[
-                    pl.ds((s * blocks + b) * picked_rows + t, per, stride=tiles), :
-                ]
-
-    def taper(b, c):
-        row_b, col_b = obs_place(owner[b], location[pl.ds(b, 1), :], cols_all, lines)
-        row_c, col_c = obs_place(owner[c], location[pl.ds(c, 1), :], cols_all, lines)
-        row_b, col_b = down(row_b, count), down(col_b, count)
-        inv_row, inv_col = inverse_of(widths[b, 0]), inverse_of(widths[b, 1])
-        return across(row_c, lambda x: ring_taper(row_b, x, float(rows_all), inv_row)) * across(
-            col_c, lambda x: ring_taper(col_b, x, float(cols_all), inv_col)
+    stride = gathered.shape[0] // senders
+    for b in range(1, blocks):
+        unpack(
+            gathered, skip + (b - 1) * picked_rows, senders, stride, members // senders, tiles, pred, b
         )
+    anom_out[0] = anom_first[...]
+    weight_out[0] = weight_first[...]
 
     def block(b, carry):
+        def earlier(a, carry):
+            now = pred[b]
+            left = stacked(anom_out[a]).T.astype(bf16)
+            cross = dot_stacked(left, anomaly(now)) * (1.0 / (members - 1))
+            pred[b] = now + dot_split(weight_out[a], obs_taper(owner, widths, location, a, b, extents, lines) * cross)
+            return carry
+
+        lax.fori_loop(0, b, earlier, 0)
         now = pred[b]
-        anom = now - jnp.sum(now, axis=0, keepdims=True) * (1.0 / members)
-        anom_out[b] = anom
-        spread = dot_exact(anom.T, anom) * scale
-        diag = lax.broadcasted_iota(jnp.int32, (count, count), 0) == lax.broadcasted_iota(
-            jnp.int32, (count, count), 1
+        anom_out[b], weight_out[b] = weights_of(
+            now,
+            obs_taper(owner, widths, location, b, b, extents, lines),
+            values[pl.ds(b, 1), :] + noise[b] - now,
+            variance[pl.ds(b, 1), :],
+            zero[...],
+            cov,
+            rhs,
         )
-        cov[...] = taper(b, b) * spread + jnp.where(diag, variance[pl.ds(b, 1), :], 0.0)
-        rhs[...] = values[pl.ds(b, 1), :] + noise[b] - now
-        corner = cov[0:LANES, 0:LANES]
-        for k in range(tiles):
-            at = slice(k * LANES, (k + 1) * LANES)
-            inv = inverse_128(corner, zeros)
-            if k + 1 < tiles:
-                after = slice((k + 1) * LANES, count)
-                soon = slice((k + 1) * LANES, (k + 2) * LANES)
-                low_soon = dot_exact(cov[soon, at], inv)
-                corner = cov[soon, soon] - dot_exact(low_soon, cov[at, soon])
-                if k + 2 < tiles:
-                    late = slice((k + 2) * LANES, count)
-                    low_late = dot_exact(cov[late, at], inv)
-                    cov[soon, late] -= dot_exact(low_soon, cov[at, late])
-                    cov[late, after] -= dot_exact(low_late, cov[at, after])
-                    cov[late, at] = low_late
-                top = dot_exact(rhs[:, at], inv)
-                rhs[:, at] = top
-                rhs[:, after] -= dot_exact(top, cov[at, after])
-                cov[soon, at] = low_soon
-            else:
-                rhs[:, at] = dot_exact(rhs[:, at], inv)
-        for k in reversed(range(tiles - 1)):
-            at = slice(k * LANES, (k + 1) * LANES)
-            after = slice((k + 1) * LANES, count)
-            rhs[:, at] -= dot_exact(rhs[:, after], cov[after, at])
-        weight = rhs[...]
-        weight_out[b] = weight
-
-        def later(c, carry):
-            now = pred[c]
-            anom_c = now - jnp.sum(now, axis=0, keepdims=True) * (1.0 / members)
-            left = stacked(anom_out[b]).T.astype(bf16)
-            cross = taper(b, c) * (dot_stacked(left, anom_c) * scale)
-            pred[c] = now + dot_split(weight_out[b], cross)
-            return carry
-
-        lax.fori_loop(b + 1, blocks, later, 0)
         return carry
 
-    lax.fori_loop(0, blocks, block, 0)
-
-
-def solve(owner, widths, gathered, location, values, noise, variance, extents, lines, picked_rows):
-    blocks, members, count = noise.shape
-    out = jax.ShapeDtypeStruct((blocks, members, count), f32)
+    lax.fori_loop(1, blocks, block, 0)
+
+
+def solve(kernel, blocks_out, args, count, members, **sizes):
+    scratch = blocks_out[0] if blocks_out else 1
 
     def body(*refs):
-        solve_kernel(*refs, extents=extents, lines=lines, picked_rows=picked_rows)
+        kernel(*refs, **sizes)
 
     return pl.pallas_call(
         body,
-        out_shape=[out, out],
-        in_specs=[smem, smem] + [vmem] * 6,
-        out_specs=[vmem, vmem],
+        out_shape=[jax.ShapeDtypeStruct(blocks_out + (members, count), f32)] * 2,
+        in_specs=[smem] * 2 + [vmem] * (len(args) - 2),
+        out_specs=[vmem] * 2,
         scratch_shapes=[
-            pltpu.VMEM((blocks, members, count), f32),
+            pltpu.VMEM((scratch, members, count), f32),
             pltpu.VMEM((count, count), f32),
             pltpu.VMEM((members, count), f32),
         ],
         compiler_params=params,
         name="solve",
-    )(owner, widths, gathered, location, values, noise, variance, jnp.zeros((GROUP, LANES), f32))
-
-
-def update_kernel(owner, widths, my_row, state, location, anom, weight, out, *, extents, lines):
+    )(*args)
+
+
+def update_kernel(
+    owner, widths, my_row, state, location, anom, weight, out, *, extents, lines, senders
+):
     rows_all, cols_all = extents
     blocks, members, count = anom.shape
-    tiles = state.shape[0] // members
-    for t in range(tiles):
-        out[:, t * LANES : (t + 1) * LANES] = state[pl.ds(t, members, stride=tiles), :]
+    tiles = cols_all // LANES
+    per = members // senders
+    stride = state.shape[0] // senders
+    for s in range(senders):
+        for t in range(tiles):
+            out[s * per : (s + 1) * per, t * LANES : (t + 1) * LANES] = state[
+                pl.ds(s * stride + t, per, stride=tiles), :
+            ]
     row = my_row[0].astype(f32)
     for b in range(blocks):
         now = out[...]
-        centered = now - jnp.sum(now, axis=0, keepdims=True) * (1.0 / members)
-        cross = dot_stacked(stacked(anom[b]).T.astype(bf16), centered)
+        cross = dot_stacked(stacked(anom[b]).T.astype(bf16), anomaly(now))
         obs_row, obs_col = obs_place(owner[b], location[b : b + 1, :], cols_all, lines)
         obs_col = down(obs_col, count)
-        lane = lax.broadcasted_iota(jnp.int32, (1, tiles * LANES), 1).astype(f32)
+        lane = lax.broadcasted_iota(jnp.int32, (1, cols_all), 1).astype(f32)
         inv_row, inv_col = inverse_of(widths[b, 0]), inverse_of(widths[b, 1])
         by_row = across(obs_row, lambda x: ring_taper(row, x, float(rows_all), inv_row))
         by_col = across(lane, lambda x: ring_taper(obs_col, x, float(cols_all), inv_col))
         out[...] = now + dot_split(weight[b] * (by_row * (1.0 / (members - 1))), by_col * cross)
 
 
-def update(owner, widths, my_row, state, location, anom, weight, extents, lines):
-    blocks, members, count = anom.shape
-    tiles = state.shape[0] // members
+def update(owner, widths, my_row, state, location, anom, weight, extents, lines, senders):
+    members = anom.shape[1]
 
     def body(*refs):
-        update_kernel(*refs, extents=extents, lines=lines)
+        update_kernel(*refs, extents=extents, lines=lines, senders=senders)
 
     return pl.pallas_call(
         body,
-        out_shape=jax.ShapeDtypeStruct((members, tiles * LANES), f32),
+        out_shape=jax.ShapeDtypeStruct((members, extents[1]), f32),
         in_specs=[smem] * 3 + [vmem] * 4,
         out_specs=vmem,
         compiler_params=params,
@@ -403,20 +462,34 @@
     )(owner, widths, my_row, state, location, anom, weight)
 
 
-def choose_kernel(owner, received, out):
-    for b in range(out.shape[0]):
-        out[b] = received[owner[b]]
-
-
-def choose(owner, received):
+def choose_kernel(owner, received, state, first, second):
+    receivers, rows, _ = first.shape
+    own_rows = state.shape[0] // receivers
+    blocks = owner.shape[0]
+    chunk = [received[owner[b]] for b in range(blocks)]
+    for m in range(receivers):
+        first[m] = chunk[0]
+        second[m, 0:own_rows, :] = state[m * own_rows : (m + 1) * own_rows, :]
+        for b in range(1, blocks):
+            at = own_rows + (b - 1) * rows
+            second[m, at : at + rows, :] = chunk[b]
+
+
+def choose(owner, received, state, receivers):
+    rows = received.shape[1]
+    blocks = owner.shape[0]
+    own_rows = state.shape[0] // receivers
     return pl.pallas_call(
         choose_kernel,
-        out_shape=jax.ShapeDtypeStruct(owner.shape + received.shape[1:], f32),
-        in_specs=[smem, vmem],
-        out_specs=vmem,
+        out_shape=[
+            jax.ShapeDtypeStruct((receivers, rows, LANES), f32),
+            jax.ShapeDtypeStruct((receivers, own_rows + (blocks - 1) * rows, LANES), f32),
+        ],
+        in_specs=[smem, vmem, vmem],
+        out_specs=[vmem, vmem],
         compiler_params=params,
         name="choose",
-    )(owner, received)
+    )(owner, received, state)
 
 
 def shards(
@@ -435,27 +508,33 @@
     above = lax.ppermute(starting_sample_set, "reg", forth)
     below = lax.ppermute(starting_sample_set, "reg", back)
 
-    mine = jnp.argmax((block_owner == region).astype(jnp.int32))
-    loc = lax.dynamic_slice_in_dim(obs_location, mine, 1, axis=0)
-    state, picked = forecast(above, starting_sample_set, below, loc, regions)
+    loc, own = prepare(block_owner, region.reshape(1), obs_location, starting_sample_set)
+    state, picked = forecast(above, own, below, loc, regions)
 
     picked_rows = picked.shape[0] // regions
     picked = lax.all_to_all(
         picked.reshape(regions, picked_rows, LANES), "reg", 0, 0, tiled=True
     )
-    gathered = lax.all_gather(choose(block_owner, picked), "mem").reshape(-1, LANES)
-
-    state = lax.all_to_all(
-        state.reshape(senders, members * GROUP, LANES), "mem", 0, 0, tiled=True
-    ).reshape(senders * members * GROUP, LANES)
-
+    skip = members * GROUP
+    first, second = choose(block_owner, picked, state, senders)
+    first = lax.all_to_all(first, "mem", 0, 0, tiled=True)
+    first, second = lax.optimization_barrier((first, second))
+    second = lax.all_to_all(second, "mem", 0, 0, tiled=True).reshape(-1, LANES)
+
+    zero = jnp.zeros((GROUP, LANES), f32)
+    sizes = dict(count=obs_location.shape[1], members=obs_noise.shape[1], senders=senders)
+    sizes.update(extents=extents, lines=lines)
+    common = (obs_location, obs_values, obs_noise, obs_variance, zero)
+    done = solve(
+        first_kernel, (), (block_owner, taper_pairs, first.reshape(-1, LANES)) + common, **sizes
+    )
     anom, weight = solve(
-        block_owner, taper_pairs, gathered, obs_location, obs_values, obs_noise, obs_variance,
-        extents, lines, picked_rows,
+        rest_kernel, block_owner.shape, (block_owner, taper_pairs, second) + common + tuple(done),
+        skip=skip, picked_rows=picked_rows, **sizes,
     )
     my_row = (region * lines + mem_index % lines).reshape(1)
     return update(
-        block_owner, taper_pairs, my_row, state, obs_location, anom, weight, extents, lines
+        block_owner, taper_pairs, my_row, second, obs_location, anom, weight, extents, lines, senders
     )
 
 

time: 133 us -> 131 us (0.985)
  starting transfers between devices: 24.9 us -> 13.8 us
  waiting for transfers between devices: 1.01 us -> 7.07 us
  blocking collectives: 44.7 us -> 48.1 us
  Pallas kernels: 56.6 us -> 58.8 us
  between operations: 2 us -> 0.13 us
  other arithmetic: 1.37 us -> 0 us
    all_to_all x0 -> x1, blocking collectives: none -> 24.9 us  [shards(): first = lax.all_to_all(first, 'mem', 0, 0, tiled=True)]
    all_gather x1 -> x0, blocking collectives: 21.4 us -> none  [shards(): lax.all_gather(choose(block_owner, picked), 'mem').reshape(-1, LANES)]
    all_to_all x1, starting transfers between devices: 14.7 us -> 3.81 us  [shards(): second = lax.all_to_all(second, 'mem', 0, 0, tiled=True).reshape(-1, LANES)]
    all_to_all x1, waiting for transfers between devices: 0.01 us -> 5.67 us  [shards(): second = lax.all_to_all(second, 'mem', 0, 0, tiled=True).reshape(-1, LANES)]
    pallas_call x3 -> x5, Pallas kernels: 51.6 us -> 53.8 us  [the longest x2 46.5 us: solve(): pl.pallas_call(body, out_shape=[jax.ShapeDtypeStruct(blocks_out + (member...]
    another operation x1 -> x0, other arithmetic: 1.37 us -> none  [shards(): mine = jnp.argmax((block_owner == region).astype(jnp.int32))]
    unnamed x15 -> x17, local copies, waits for them, and re-layouts: 2.41 us -> 3.02 us
  transfers between devices with their start and end apart: 3 -> 3, of which waited for: 1 -> 2; matrix products, arithmetic and copies ran while one was open for 1% -> 0% of each run, Pallas kernels for 35% -> 11%
where the time goes in v3:
time: 131 us
  Pallas kernels  58.8 us (45%)
  blocking collectives  48.1 us (37%)
  starting transfers between devices  13.8 us (11%)
  waiting for transfers between devices  7.07 us (5%)
  local copies, waits for them, and re-layouts  3.02 us (2%)
    pallas_call x2, Pallas kernels, solve(): pl.pallas_call(body, out_shape=[jax.ShapeDtypeStruct(blocks_out + (member...  46.5 us
    all_to_all x1, blocking collectives, shards(): first = lax.all_to_all(first, 'mem', 0, 0, tiled=True)  24.9 us
    all_to_all x1, blocking collectives, shards(): lax.all_to_all(picked.reshape(regions, picked_rows, LANES), 'reg', 0, 0,...  23.3 us
    ppermute x1, starting transfers between devices, shards(): below = lax.ppermute(starting_sample_set, 'reg', back)  6.09 us
    all_to_all x1, waiting for transfers between devices, shards(): second = lax.all_to_all(second, 'mem', 0, 0, tiled=True).reshape(-1, LANES)  5.67 us
    pallas_call x1, Pallas kernels, update(): pl.pallas_call(body, out_shape=jax.ShapeDtypeStruct((members, extents[1])...  5.2 us
    pallas_call x1, Pallas kernels, forecast(): pl.pallas_call(body, out_shape=[jax.ShapeDtypeStruct((n_dest * members *...  4.99 us
    ppermute x1, starting transfers between devices, shards(): above = lax.ppermute(starting_sample_set, 'reg', forth)  3.94 us
  transfers between devices with their start and end apart: 3, of which 2 were waited for; matrix products, arithmetic and copies ran while one was open for 0% of the time, Pallas kernels for 11%

profile of v3, /device:TPU:1, one launch (start us, length us, event | category | flops | bytes accessed | tf_op | source)
XLA Modules:
  0.0 130.9 jit_solution(7922694657857933332)
XLA Ops:
  0.0 3.9 %collective-permute-start = (f32[5,4,4,1024]{3,2,1,0:T(4,128)}, f32[5,4,4,1024]{3,2,1,0:T(4,128)S(1)}, u32[]{:S(2)}, u32[]{:S(2)}) collective-permute-start(f32[5,4,4,1024]{3,2,1,0:T(4,128)} %own.1), channel_id=1, source_target_pairs={{0,1},{1,2},{2,3},{3,4},{4,5},{5,6},{6,7},{7,8},{8,9},{9,10},{10,1... | collective-permute-start | bytes 983048 | tf_op jit(solution)/shard_map/ppermute | solution.py:508
  3.9 6.1 %collective-permute-start.1 = (f32[5,4,4,1024]{3,2,1,0:T(4,128)}, f32[5,4,4,1024]{3,2,1,0:T(4,128)S(1)}, u32[]{:S(2)}, u32[]{:S(2)}) collective-permute-start(f32[5,4,4,1024]{3,2,1,0:T(4,128)} %own.1), channel_id=1, source_target_pairs={{1,0},{2,1},{3,2},{4,3},{5,4},{6,5},{7,6},{8,7},{9,8},{10,9},{11,1... | collective-permute-start | bytes 983048 | tf_op jit(solution)/shard_map/ppermute | solution.py:509
  10.0 0.0 copy-start.6
  10.1 0.6 copy-done.6
  10.7 0.0 copy-start.1
  10.7 1.0 copy-done.1
  11.7 0.0 copy-start.2
  11.7 0.7 copy-done.2
  12.4 0.6 prepare.1
  12.9 0.0 collective-permute-done.refs_0_
  13.0 1.4 %collective-permute-done.1.refs_2_ = f32[5,4,4,1024]{3,2,1,0:T(4,128)S(1)} collective-permute-done((f32[5,4,4,1024]{3,2,1,0:T(4,128)}, f32[5,4,4,1024]{3,2,1,0:T(4,128)S(1)}, u32[]{:S(2)}, u32[]{:S(2)}) %collective-permute-start.1) | collective-permute-done | bytes 327712 | tf_op jit(solution)/shard_map/ppermute | solution.py:509
  14.4 5.0 %forecast.1 = (f32[640,128]{1,0:T(8,128)S(1)}, f32[768,128]{1,0:T(8,128)S(1)}) custom-call(f32[5,4,4,1024]{3,2,1,0:T(4,128)S(1)} %collective-permute-done.refs_0_, f32[5,4,4,1024]{3,2,1,0:T(4,128)S(1)} %get-tuple-element.17.refs_1_, f32[5,4,4,1024]{3,2,1,0:T(4,128)S(1)} %collective-permute-done.1.refs_2_, s32[1,512]{1,0:T(1,128)S(1)} %get-tuple-element.18.refs_3_), custom_call_target="tpu_custom_call" | custom-call | tf_op jit(solution)/shard_map/forecast/pallas_call | solution.py:158
  19.4 23.3 %all_to_all.15.received = f32[32,24,128]{2,1,0:T(8,128)S(1)} all-to-all(f32[32,24,128]{2,1,0:T(8,128)S(1)} %bitcast.8), channel_id=1, replica_groups=mesh['mem'=16,'reg'=32] {'reg'}, dimensions={0} | all-to-all | bytes 786432 | tf_op jit(solution)/shard_map/all_to_all | solution.py:515
  42.6 1.5 %choose.1 = (f32[16,24,128]{2,1,0:T(8,128)S(1)}, f32[16,88,128]{2,1,0:T(8,128)}) custom-call(s32[3]{0:T(128)S(1)} %copy-done.6, f32[32,24,128]{2,1,0:T(8,128)S(1)} %all_to_all.15.received, f32[640,128]{1,0:T(8,128)S(1)} %get-tuple-element.20.state), custom_call_target="tpu_custom_call" | custom-call | tf_op jit(solution)/shard_map/choose/pallas_call | solution.py:482
  44.1 24.9 %all_to_all.16 = f32[16,24,128]{2,1,0:T(8,128)S(1)} all-to-all(f32[16,24,128]{2,1,0:T(8,128)S(1)} %get-tuple-element.21), channel_id=1, replica_groups=mesh['mem'=16,'reg'=32] {'mem'}, dimensions={0} | all-to-all | bytes 393216 | tf_op jit(solution)/shard_map/all_to_all | solution.py:520
  68.9 0.0 copy-start.7
  68.9 0.0 copy-start
  69.0 3.8 %all-to-all-start.2 = ((f32[16,88,128]{2,1,0:T(8,128)}), f32[16,88,128]{2,1,0:T(8,128)S(1)}, u32[]{:S(2)}, u32[]{:S(2)}) async-start(f32[16,88,128]{2,1,0:T(8,128)} %get-tuple-element.23), calls=%async_computation.2 | async-start | bytes 1441792 | tf_op jit(solution)/shard_map/all_to_all | solution.py:522
  72.8 0.0 copy-start.5
  72.8 0.0 copy-start.4
  72.8 0.0 copy-done.7
  72.8 0.0 copy-start.3
  72.8 0.1 copy.10.refs_1_
  72.9 0.0 copy-done
  72.9 0.5 copy-done.5
  73.5 0.0 copy-done.4
  73.5 0.0 copy-done.3
  73.5 14.3 %solve.2 = (f32[80,512]{1,0:T(8,128)S(1)}, f32[80,512]{1,0:T(8,128)S(1)}) custom-call(s32[3]{0:T(128)S(1)} %copy-done.6, s32[3,2]{1,0:T(4,128)S(1)} %copy.10.refs_1_, f32[384,128]{1,0:T(8,128)S(1)} %bitcast.7, s32[3,512]{1,0:T(4,128)S(1)} %copy-done.3, f32[3,512]{1,0:T(4,128)S(1)} %copy-done.4, f32[3,80,512]{2,1,0:T(8,128)S(1)} %copy-done, ...), custom_call_target="tpu_custom_call" | custom-call | tf_op jit(solution)/shard_map/solve/pallas_call | solution.py:408
  87.8 5.7 %all-to-all-done.2 = f32[16,88,128]{2,1,0:T(8,128)S(1)} async-done(((f32[16,88,128]{2,1,0:T(8,128)}), f32[16,88,128]{2,1,0:T(8,128)S(1)}, u32[]{:S(2)}, u32[]{:S(2)}) %all-to-all-start.2) | async-done | bytes 720928 | tf_op jit(solution)/shard_map/all_to_all | solution.py:522
  93.5 32.2 %solve.3 = (f32[3,80,512]{2,1,0:T(8,128)S(1)}, f32[3,80,512]{2,1,0:T(8,128)S(1)}) custom-call(s32[3]{0:T(128)S(1)} %copy-done.6, s32[3,2]{1,0:T(4,128)S(1)} %copy.10.refs_1_, f32[1408,128]{1,0:T(8,128)S(1)} %bitcast.5, s32[3,512]{1,0:T(4,128)S(1)} %copy-done.3, f32[3,512]{1,0:T(4,128)S(1)} %copy-done.4, f32[3,80,512]{2,1,0:T(8,128)S(1)} %copy-done, ...), custom_call_target="tpu_custom_call" | custom-call | tf_op jit(solution)/shard_map/solve/pallas_call | solution.py:408
  125.7 5.2 %update.1 = f32[80,1024]{1,0:T(8,128)} custom-call(s32[3]{0:T(128)S(1)} %copy-done.6, s32[3,2]{1,0:T(4,128)S(1)} %copy.10.refs_1_, s32[1]{0:T(128)} %bitcast.refs_2_, f32[1408,128]{1,0:T(8,128)S(1)} %bitcast.6, s32[3,512]{1,0:T(4,128)S(1)} %copy-done.3, f32[3,80,512]{2,1,0:T(8,128)S(1)} %get-tuple-element.27.refs_5_, f32[3,80,512]{2,1,0:T(8,128)S(1)} %get-tuple-element.28.refs_6_), custom_call_target="tpu_custom_call" | custom-call | tf_op jit(solution)/shard_map/update/pallas_call | solution.py:455
  (1 shorter events, 0.0 us)
Async XLA Ops:
  0.0 12.9 %collective-permute-start = (f32[5,4,4,1024]{3,2,1,0:T(4,128)}, f32[5,4,4,1024]{3,2,1,0:T(4,128)S(1)}, u32[]{:S(2)}, u32[]{:S(2)}) collective-permute-start(f32[5,4,4,1024]{3,2,1,0:T(4,128)} %own.1), channel_id=1, source_target_pairs={{0,1},{1,2},{2,3},{3,4},{4,5},{5,6},{6,7},{7,8},{8,9},{9,10},{10,1... | collective-permute-start | bytes 983048 | tf_op jit(solution)/shard_map/ppermute | solution.py:508
  3.9 10.4 %collective-permute-start.1 = (f32[5,4,4,1024]{3,2,1,0:T(4,128)}, f32[5,4,4,1024]{3,2,1,0:T(4,128)S(1)}, u32[]{:S(2)}, u32[]{:S(2)}) collective-permute-start(f32[5,4,4,1024]{3,2,1,0:T(4,128)} %own.1), channel_id=1, source_target_pairs={{1,0},{2,1},{3,2},{4,3},{5,4},{6,5},{7,6},{8,7},{9,8},{10,9},{11,1... | collective-permute-start | bytes 983048 | tf_op jit(solution)/shard_map/ppermute | solution.py:509
  10.0 0.7 copy-start.6
  10.7 1.0 copy-start.1
  11.7 0.7 copy-start.2
  68.9 3.9 %copy-start.7 = (s32[3,2]{0,1:T(2,128)S(1)}, s32[3,2]{0,1:T(2,128)}, u32[]{:S(2)}) copy-start(s32[3,2]{0,1:T(2,128)} %param.10) | copy-start | bytes 76
  68.9 4.0 %copy-start = (f32[3,80,512]{2,1,0:T(8,128)S(1)}, f32[3,80,512]{2,1,0:T(8,128)}, u32[]{:S(2)}) copy-start(f32[3,80,512]{2,1,0:T(8,128)} %refs_5_.3) | copy-start | bytes 1474564
  69.0 24.6 %all-to-all-start.2 = ((f32[16,88,128]{2,1,0:T(8,128)}), f32[16,88,128]{2,1,0:T(8,128)S(1)}, u32[]{:S(2)}, u32[]{:S(2)}) async-start(f32[16,88,128]{2,1,0:T(8,128)} %get-tuple-element.23), calls=%async_computation.2 | async-start | bytes 1441792 | tf_op jit(solution)/shard_map/all_to_all | solution.py:522
  72.8 0.7 copy-start.5
  72.8 0.7 copy-start.4
  72.8 0.7 copy-start.3

commit v4 on v3

--- a/solution.py
+++ b/solution.py
@@ -86,9 +86,13 @@
 
     def member(m, carry):
         c = [rows[m, f] for f in range(fields)]
-        for _ in range(STEPS):
+        first = 0
+        for step in range(STEPS):
+            if 3 * lines - 2 * step == GROUP:
+                c = [x[step : step + GROUP] for x in c]
+                first = step
             n = [pltpu.roll(x, 1, 0) for x in c]
-            s = [pltpu.roll(x, pad - 1, 0) for x in c]
+            s = [pltpu.roll(x, x.shape[0] - 1, 0) for x in c]
             w = [pltpu.roll(x, 1, 1) for x in c]
             e = [pltpu.roll(x, width - 1, 1) for x in c]
             smooth = [
@@ -110,7 +114,7 @@
                 smooth[3] - COURANT * carried[3],
             ]
         for f in range(fields):
-            mine = c[f][lines : 2 * lines]
+            mine = c[f][lines - first : 2 * lines - first]
             for t in range(width // LANES):
                 at = t * n_rows + f * lines * GROUP + m
                 columns[pl.ds(at, lines, stride=GROUP), :] = mine[:, t * LANES : (t + 1) * LANES]
@@ -194,22 +198,22 @@
             for i, g in enumerate(own)
         ]
     )
+    scale = [None] * PANEL
     for j in range(width):
         mine, at = divmod(j, GROUP)
+        pivot = sub == at
         inv = pltpu.reciprocal(row_bcast(col[j][mine], at))
-        pivot = sub == at
+        scale[mine] = inv if scale[mine] is None else jnp.where(pivot, inv, scale[mine])
         coef = list(col[j])
-        coef[mine] = jnp.where(pivot, -1.0, coef[mine])
+        coef[mine] = jnp.where(pivot, 0.0, coef[mine])
         for k in range(j + 1, width + 1):
             row = row_bcast(col[k][mine], at)
-            old = list(col[k])
-            old[mine] = jnp.where(pivot, 0.0, old[mine])
             if k == j + 1:
-                col[k] = [old[g] - (coef[g] * row) * inv for g in range(PANEL)]
+                col[k] = [col[k][g] - (coef[g] * row) * inv for g in range(PANEL)]
             else:
                 row = row * inv
-                col[k] = [old[g] - coef[g] * row for g in range(PANEL)]
-    panel = col[width]
+                col[k] = [col[k][g] - coef[g] * row for g in range(PANEL)]
+    panel = [col[width][g] * scale[g] for g in range(PANEL)]
     out = list(m)
     for i, g in enumerate(own):
         out[g] = panel[i]
@@ -302,15 +306,15 @@
     return x - jnp.sum(x, axis=0, keepdims=True) * (1.0 / x.shape[0])
 
 
-def unpack(gathered, first, senders, stride, per, tiles, out, b):
+def unpack(gathered, first, senders, stride, per, tiles, out):
     for s in range(senders):
         for t in range(tiles):
-            out[b, s * per : (s + 1) * per, t * LANES : (t + 1) * LANES] = gathered[
+            out[s * per : (s + 1) * per, t * LANES : (t + 1) * LANES] = gathered[
                 pl.ds(s * stride + first + t, per, stride=tiles), :
             ]
 
 
-def weights_of(now, taper, misfit, variance, zeros, cov, rhs):
+def weights_of(now, taper, misfit, variance, zeros, cov, rhs, beside=lambda k: None):
     members, count = now.shape
     tiles = count // LANES
     anom = anomaly(now)
@@ -322,29 +326,31 @@
     rhs[...] = misfit
     corner = cov[0:LANES, 0:LANES]
     for k in range(tiles):
+        before = slice(0, k * LANES)
         at = slice(k * LANES, (k + 1) * LANES)
+        after = slice((k + 1) * LANES, count)
         inv = inverse_128(corner, zeros)
         if k + 1 < tiles:
-            after = slice((k + 1) * LANES, count)
             soon = slice((k + 1) * LANES, (k + 2) * LANES)
             low_soon = dot_exact(cov[soon, at], inv)
             corner = cov[soon, soon] - dot_exact(low_soon, cov[at, soon])
+            low = low_soon
             if k + 2 < tiles:
                 late = slice((k + 2) * LANES, count)
                 low_late = dot_exact(cov[late, at], inv)
                 cov[soon, late] -= dot_exact(low_soon, cov[at, late])
                 cov[late, after] -= dot_exact(low_late, cov[at, after])
-                cov[late, at] = low_late
-            top = dot_exact(rhs[:, at], inv)
-            rhs[:, at] = top
+                low = jnp.concatenate([low_soon, low_late], axis=0)
+        top = dot_exact(rhs[:, at], inv)
+        rhs[:, at] = top
+        if k + 1 < tiles:
             rhs[:, after] -= dot_exact(top, cov[at, after])
-            cov[soon, at] = low_soon
-        else:
-            rhs[:, at] = dot_exact(rhs[:, at], inv)
-    for k in reversed(range(tiles - 1)):
-        at = slice(k * LANES, (k + 1) * LANES)
-        after = slice((k + 1) * LANES, count)
-        rhs[:, at] -= dot_exact(rhs[:, after], cov[after, at])
+            if k:
+                cov[after, before] -= dot_exact(low, cov[at, before])
+            cov[after, at] = low
+        if k:
+            rhs[:, before] -= dot_exact(top, cov[at, before])
+        beside(k)
     return anom, rhs[...]
 
 
@@ -354,38 +360,63 @@
 ):
     members, count = anom_out.shape
     taper = obs_taper(owner, widths, location, 0, 0, extents, lines)
-    unpack(gathered, 0, senders, gathered.shape[0] // senders, members // senders, count // LANES, pred, 0)
-    now = pred[0]
+    stride = gathered.shape[0] // senders
+    unpack(gathered, 0, senders, stride, members // senders, count // LANES, pred)
+    now = pred[...]
     anom_out[...], weight_out[...] = weights_of(
         now, taper, values[0:1, :] + noise[0] - now, variance[0:1, :], zero[...], cov, rhs
     )
 
 
 def rest_kernel(
-    owner, widths, gathered, location, values, noise, variance, zero, anom_first, weight_first,
-    anom_out, weight_out, pred, cov, rhs, *, senders, extents, lines, skip, picked_rows
+    owner, widths, gathered, location, values, noise, variance, zero, anom_first, weight_first, my_row,
+    out, anom_all, weight_all, pred, cov, rhs, *, senders, extents, lines, skip, picked_rows
 ):
+    rows_all, cols_all = extents
     blocks, members, count = noise.shape
-    tiles = count // LANES
+    per = members // senders
     stride = gathered.shape[0] // senders
     for b in range(1, blocks):
         unpack(
-            gathered, skip + (b - 1) * picked_rows, senders, stride, members // senders, tiles, pred, b
+            gathered, skip + (b - 1) * picked_rows, senders, stride, per, count // LANES, pred.at[b]
         )
-    anom_out[0] = anom_first[...]
-    weight_out[0] = weight_first[...]
+    unpack(gathered, 0, senders, stride, per, cols_all // LANES, out)
+    anom_all[0] = anom_first[...]
+    weight_all[0] = weight_first[...]
+    row = my_row[0].astype(f32)
+    share = 1.0 / (members - 1)
+
+    def own_variables(b):
+        obs_row, obs_col = obs_place(owner[b], location[pl.ds(b, 1), :], cols_all, lines)
+        inv_row, inv_col = inverse_of(widths[b, 0]), inverse_of(widths[b, 1])
+        left = stacked(anom_all[b]).T.astype(bf16)
+        by_row = across(obs_row, lambda x: ring_taper(row, x, float(rows_all), inv_row))
+        weight = weight_all[b] * (by_row * share)
+        obs_col = down(obs_col, count)
+
+        def part(k, parts=count // LANES):
+            size = cols_all // parts
+            at = slice(k * size, (k + 1) * size)
+            now = out[:, at]
+            cross = dot_stacked(left, anomaly(now))
+            lane = lax.broadcasted_iota(jnp.int32, (1, size), 1).astype(f32) + float(k * size)
+            by_col = across(lane, lambda x: ring_taper(obs_col, x, float(cols_all), inv_col))
+            out[:, at] = now + dot_split(weight, by_col * cross)
+
+        return part
 
     def block(b, carry):
         def earlier(a, carry):
             now = pred[b]
-            left = stacked(anom_out[a]).T.astype(bf16)
-            cross = dot_stacked(left, anomaly(now)) * (1.0 / (members - 1))
-            pred[b] = now + dot_split(weight_out[a], obs_taper(owner, widths, location, a, b, extents, lines) * cross)
+            left = stacked(anom_all[a]).T.astype(bf16)
+            cross = dot_stacked(left, anomaly(now)) * share
+            taper = obs_taper(owner, widths, location, a, b, extents, lines)
+            pred[b] = now + dot_split(weight_all[a], taper * cross)
             return carry
 
         lax.fori_loop(0, b, earlier, 0)
         now = pred[b]
-        anom_out[b], weight_out[b] = weights_of(
+        anom, weight = weights_of(
             now,
             obs_taper(owner, widths, location, b, b, extents, lines),
             values[pl.ds(b, 1), :] + noise[b] - now,
@@ -393,77 +424,34 @@
             zero[...],
             cov,
             rhs,
+            own_variables(b - 1),
         )
+        anom_all[b] = anom
+        weight_all[b] = weight
         return carry
 
     lax.fori_loop(1, blocks, block, 0)
-
-
-def solve(kernel, blocks_out, args, count, members, **sizes):
-    scratch = blocks_out[0] if blocks_out else 1
-
+    own_variables(blocks - 1)(0, 1)
+
+
+def solve(kernel, args, outs, scratch, count, members, **sizes):
     def body(*refs):
         kernel(*refs, **sizes)
 
     return pl.pallas_call(
         body,
-        out_shape=[jax.ShapeDtypeStruct(blocks_out + (members, count), f32)] * 2,
-        in_specs=[smem] * 2 + [vmem] * (len(args) - 2),
-        out_specs=[vmem] * 2,
-        scratch_shapes=[
-            pltpu.VMEM((scratch, members, count), f32),
-            pltpu.VMEM((count, count), f32),
-            pltpu.VMEM((members, count), f32),
-        ],
+        out_shape=[jax.ShapeDtypeStruct(shape, f32) for shape in outs],
+        in_specs=[smem] * 2 + [vmem] * 8 + [smem] if len(args) == 11 else [smem] * 2 + [vmem] * 6,
+        out_specs=[vmem] * len(outs),
+        scratch_shapes=[pltpu.VMEM(shape, f32) for shape in scratch]
+        + [pltpu.VMEM((count, count), f32), pltpu.VMEM((members, count), f32)],
         compiler_params=params,
         name="solve",
     )(*args)
 
 
-def update_kernel(
-    owner, widths, my_row, state, location, anom, weight, out, *, extents, lines, senders
-):
-    rows_all, cols_all = extents
-    blocks, members, count = anom.shape
-    tiles = cols_all // LANES
-    per = members // senders
-    stride = state.shape[0] // senders
-    for s in range(senders):
-        for t in range(tiles):
-            out[s * per : (s + 1) * per, t * LANES : (t + 1) * LANES] = state[
-                pl.ds(s * stride + t, per, stride=tiles), :
-            ]
-    row = my_row[0].astype(f32)
-    for b in range(blocks):
-        now = out[...]
-        cross = dot_stacked(stacked(anom[b]).T.astype(bf16), anomaly(now))
-        obs_row, obs_col = obs_place(owner[b], location[b : b + 1, :], cols_all, lines)
-        obs_col = down(obs_col, count)
-        lane = lax.broadcasted_iota(jnp.int32, (1, cols_all), 1).astype(f32)
-        inv_row, inv_col = inverse_of(widths[b, 0]), inverse_of(widths[b, 1])
-        by_row = across(obs_row, lambda x: ring_taper(row, x, float(rows_all), inv_row))
-        by_col = across(lane, lambda x: ring_taper(obs_col, x, float(cols_all), inv_col))
-        out[...] = now + dot_split(weight[b] * (by_row * (1.0 / (members - 1))), by_col * cross)
-
-
-def update(owner, widths, my_row, state, location, anom, weight, extents, lines, senders):
-    members = anom.shape[1]
-
-    def body(*refs):
-        update_kernel(*refs, extents=extents, lines=lines, senders=senders)
-
-    return pl.pallas_call(
-        body,
-        out_shape=jax.ShapeDtypeStruct((members, extents[1]), f32),
-        in_specs=[smem] * 3 + [vmem] * 4,
-        out_specs=vmem,
-        compiler_params=params,
-        name="update",
-    )(owner, widths, my_row, state, location, anom, weight)
-
-
-def choose_kernel(owner, received, state, first, second):
-    receivers, rows, _ = first.shape
+def choose_kernel(owner, received, state, first, second, *, used):
+    receivers = first.shape[0]
     own_rows = state.shape[0] // receivers
     blocks = owner.shape[0]
     chunk = [received[owner[b]] for b in range(blocks)]
@@ -471,19 +459,23 @@
         first[m] = chunk[0]
         second[m, 0:own_rows, :] = state[m * own_rows : (m + 1) * own_rows, :]
         for b in range(1, blocks):
-            at = own_rows + (b - 1) * rows
-            second[m, at : at + rows, :] = chunk[b]
-
-
-def choose(owner, received, state, receivers):
+            at = own_rows + (b - 1) * used
+            second[m, at : at + used, :] = chunk[b][:used]
+
+
+def choose(owner, received, state, receivers, used):
     rows = received.shape[1]
     blocks = owner.shape[0]
     own_rows = state.shape[0] // receivers
+
+    def body(*refs):
+        choose_kernel(*refs, used=used)
+
     return pl.pallas_call(
-        choose_kernel,
+        body,
         out_shape=[
             jax.ShapeDtypeStruct((receivers, rows, LANES), f32),
-            jax.ShapeDtypeStruct((receivers, own_rows + (blocks - 1) * rows, LANES), f32),
+            jax.ShapeDtypeStruct((receivers, own_rows + (blocks - 1) * used, LANES), f32),
         ],
         in_specs=[smem, vmem, vmem],
         out_specs=[vmem, vmem],
@@ -516,26 +508,33 @@
         picked.reshape(regions, picked_rows, LANES), "reg", 0, 0, tiled=True
     )
     skip = members * GROUP
-    first, second = choose(block_owner, picked, state, senders)
+    used = members * obs_location.shape[1] // LANES
+    first, second = choose(block_owner, picked, state, senders, used)
     first = lax.all_to_all(first, "mem", 0, 0, tiled=True)
     first, second = lax.optimization_barrier((first, second))
     second = lax.all_to_all(second, "mem", 0, 0, tiled=True).reshape(-1, LANES)
 
     zero = jnp.zeros((GROUP, LANES), f32)
-    sizes = dict(count=obs_location.shape[1], members=obs_noise.shape[1], senders=senders)
-    sizes.update(extents=extents, lines=lines)
+    my_row = (region * lines + mem_index % lines).reshape(1)
+    one = obs_noise.shape[1:]
+    sizes = dict(count=one[1], members=one[0], senders=senders, extents=extents, lines=lines)
     common = (obs_location, obs_values, obs_noise, obs_variance, zero)
     done = solve(
-        first_kernel, (), (block_owner, taper_pairs, first.reshape(-1, LANES)) + common, **sizes
-    )
-    anom, weight = solve(
-        rest_kernel, block_owner.shape, (block_owner, taper_pairs, second) + common + tuple(done),
-        skip=skip, picked_rows=picked_rows, **sizes,
-    )
-    my_row = (region * lines + mem_index % lines).reshape(1)
-    return update(
-        block_owner, taper_pairs, my_row, second, obs_location, anom, weight, extents, lines, senders
-    )
+        first_kernel,
+        (block_owner, taper_pairs, first.reshape(-1, LANES)) + common,
+        (one, one),
+        (one,),
+        **sizes,
+    )
+    return solve(
+        rest_kernel,
+        (block_owner, taper_pairs, second) + common + tuple(done) + (my_row,),
+        ((one[0], width),),
+        (obs_noise.shape,) * 3,
+        skip=skip,
+        picked_rows=used,
+        **sizes,
+    )[0]
 
 
 def solution(mesh):

time: 131 us -> 127 us (0.969)
  Pallas kernels: 58.8 us -> 56.2 us
  waiting for transfers between devices: 7.07 us -> 4.86 us
    pallas_call x4 -> x3, Pallas kernels: 53.2 us -> 50.5 us  [the longest x2 49 us: solve(): pl.pallas_call(body, out_shape=[jax.ShapeDtypeStruct(shape, f32) for shap...]
    all_to_all x1, waiting for transfers between devices: 5.67 us -> 3.46 us  [shards(): second = lax.all_to_all(second, 'mem', 0, 0, tiled=True).reshape(-1, LANES)]
where the time goes in v4:
time: 127 us; the launch traced here: 126 us
  Pallas kernels  56.2 us (44%)
  blocking collectives  48.1 us (38%)
  starting transfers between devices  13.8 us (11%)
  waiting for transfers between devices  4.86 us (4%)
  local copies, waits for them, and re-layouts  3.02 us (2%)
    pallas_call x2, Pallas kernels, solve(): pl.pallas_call(body, out_shape=[jax.ShapeDtypeStruct(shape, f32) for shap...  49 us
    all_to_all x1, blocking collectives, shards(): first = lax.all_to_all(first, 'mem', 0, 0, tiled=True)  24.8 us
    all_to_all x1, blocking collectives, shards(): lax.all_to_all(picked.reshape(regions, picked_rows, LANES), 'reg', 0, 0,...  23.3 us
    ppermute x1, starting transfers between devices, shards(): below = lax.ppermute(starting_sample_set, 'reg', back)  6.09 us
    pallas_call x1, Pallas kernels, forecast(): pl.pallas_call(body, out_shape=[jax.ShapeDtypeStruct((n_dest * members *...  5.15 us
    ppermute x1, starting transfers between devices, shards(): above = lax.ppermute(starting_sample_set, 'reg', forth)  3.94 us
    all_to_all x1, starting transfers between devices, shards(): second = lax.all_to_all(second, 'mem', 0, 0, tiled=True).reshape(-1, LANES)  3.8 us
    all_to_all x1, waiting for transfers between devices, shards(): second = lax.all_to_all(second, 'mem', 0, 0, tiled=True).reshape(-1, LANES)  3.46 us
  transfers between devices with their start and end apart: 3, of which 2 were waited for; matrix products, arithmetic and copies ran while one was open for 0% of the time, Pallas kernels for 11%

profile of v4, /device:TPU:1, one launch (start us, length us, event | category | flops | bytes accessed | tf_op | source)
XLA Modules:
  0.0 126.1 jit_solution(11906596478336720632)
XLA Ops:
  0.0 3.9 %collective-permute-start = (f32[5,4,4,1024]{3,2,1,0:T(4,128)}, f32[5,4,4,1024]{3,2,1,0:T(4,128)S(1)}, u32[]{:S(2)}, u32[]{:S(2)}) collective-permute-start(f32[5,4,4,1024]{3,2,1,0:T(4,128)} %own.1), channel_id=1, source_target_pairs={{0,1},{1,2},{2,3},{3,4},{4,5},{5,6},{6,7},{7,8},{8,9},{9,10},{10,1... | collective-permute-start | bytes 983048 | tf_op jit(solution)/shard_map/ppermute | solution.py:500
  3.9 6.1 %collective-permute-start.1 = (f32[5,4,4,1024]{3,2,1,0:T(4,128)}, f32[5,4,4,1024]{3,2,1,0:T(4,128)S(1)}, u32[]{:S(2)}, u32[]{:S(2)}) collective-permute-start(f32[5,4,4,1024]{3,2,1,0:T(4,128)} %own.1), channel_id=1, source_target_pairs={{1,0},{2,1},{3,2},{4,3},{5,4},{6,5},{7,6},{8,7},{9,8},{10,9},{11,1... | collective-permute-start | bytes 983048 | tf_op jit(solution)/shard_map/ppermute | solution.py:501
  10.0 0.0 copy-start.6
  10.1 0.6 copy-done.6
  10.7 0.0 copy-start.1
  10.7 1.0 copy-done.1
  11.7 0.0 copy-start.2
  11.7 0.7 copy-done.2
  12.4 0.6 prepare.1
  12.9 0.0 collective-permute-done.refs_0_
  13.0 1.4 %collective-permute-done.1.refs_2_ = f32[5,4,4,1024]{3,2,1,0:T(4,128)S(1)} collective-permute-done((f32[5,4,4,1024]{3,2,1,0:T(4,128)}, f32[5,4,4,1024]{3,2,1,0:T(4,128)S(1)}, u32[]{:S(2)}, u32[]{:S(2)}) %collective-permute-start.1) | collective-permute-done | bytes 327712 | tf_op jit(solution)/shard_map/ppermute | solution.py:501
  14.4 5.2 %forecast.1 = (f32[640,128]{1,0:T(8,128)S(1)}, f32[768,128]{1,0:T(8,128)S(1)}) custom-call(f32[5,4,4,1024]{3,2,1,0:T(4,128)S(1)} %collective-permute-done.refs_0_, f32[5,4,4,1024]{3,2,1,0:T(4,128)S(1)} %get-tuple-element.15.refs_1_, f32[5,4,4,1024]{3,2,1,0:T(4,128)S(1)} %collective-permute-done.1.refs_2_, s32[1,512]{1,0:T(1,128)S(1)} %get-tuple-element.16.refs_3_), custom_call_target="tpu_custom_call" | custom-call | tf_op jit(solution)/shard_map/forecast/pallas_call | solution.py:162
  19.5 23.3 %all_to_all.15.refs_1_ = f32[32,24,128]{2,1,0:T(8,128)S(1)} all-to-all(f32[32,24,128]{2,1,0:T(8,128)S(1)} %bitcast.7), channel_id=1, replica_groups=mesh['mem'=16,'reg'=32] {'reg'}, dimensions={0} | all-to-all | bytes 786432 | tf_op jit(solution)/shard_map/all_to_all | solution.py:507
  42.8 1.4 %choose.1 = (f32[16,24,128]{2,1,0:T(8,128)S(1)}, f32[16,80,128]{2,1,0:T(8,128)}) custom-call(s32[3]{0:T(128)S(1)} %copy-done.6, f32[32,24,128]{2,1,0:T(8,128)S(1)} %all_to_all.15.refs_1_, f32[640,128]{1,0:T(8,128)S(1)} %get-tuple-element.18.refs_2_), custom_call_target="tpu_custom_call" | custom-call | tf_op jit(solution)/shard_map/choose/pallas_call | solution.py:474
  44.2 24.8 %all_to_all.16 = f32[16,24,128]{2,1,0:T(8,128)S(1)} all-to-all(f32[16,24,128]{2,1,0:T(8,128)S(1)} %get-tuple-element.19), channel_id=1, replica_groups=mesh['mem'=16,'reg'=32] {'mem'}, dimensions={0} | all-to-all | bytes 393216 | tf_op jit(solution)/shard_map/all_to_all | solution.py:513
  69.1 0.0 copy-start.7
  69.1 0.0 copy-start
  69.1 3.8 %all-to-all-start.2 = ((f32[16,80,128]{2,1,0:T(8,128)}), f32[16,80,128]{2,1,0:T(8,128)S(1)}, u32[]{:S(2)}, u32[]{:S(2)}) async-start(f32[16,80,128]{2,1,0:T(8,128)} %get-tuple-element.21), calls=%async_computation.2 | async-start | bytes 1310720 | tf_op jit(solution)/shard_map/all_to_all | solution.py:515
  72.9 0.0 copy-start.5
  72.9 0.0 copy-start.4
  72.9 0.0 copy-done.7
  72.9 0.0 copy-start.3
  73.0 0.1 copy.9.refs_1_
  73.1 0.0 copy-done
  73.1 0.5 copy-done.5
  73.6 0.0 copy-done.4
  73.6 0.0 copy-done.3
  73.7 13.9 %solve.2 = (f32[80,512]{1,0:T(8,128)S(1)}, f32[80,512]{1,0:T(8,128)S(1)}) custom-call(s32[3]{0:T(128)S(1)} %copy-done.6, s32[3,2]{1,0:T(4,128)S(1)} %copy.9.refs_1_, f32[384,128]{1,0:T(8,128)S(1)} %bitcast.6, s32[3,512]{1,0:T(4,128)S(1)} %copy-done.3, f32[3,512]{1,0:T(4,128)S(1)} %copy-done.4, f32[3,80,512]{2,1,0:T(8,128)S(1)} %copy-done, ...), custom_call_target="tpu_custom_call" | custom-call | tf_op jit(solution)/shard_map/solve/pallas_call | solution.py:441
  87.6 3.5 %all-to-all-done.2 = f32[16,80,128]{2,1,0:T(8,128)S(1)} async-done(((f32[16,80,128]{2,1,0:T(8,128)}), f32[16,80,128]{2,1,0:T(8,128)S(1)}, u32[]{:S(2)}, u32[]{:S(2)}) %all-to-all-start.2) | async-done | bytes 655392 | tf_op jit(solution)/shard_map/all_to_all | solution.py:515
  91.0 35.1 %solve.3 = f32[80,1024]{1,0:T(8,128)} custom-call(s32[3]{0:T(128)S(1)} %copy-done.6, s32[3,2]{1,0:T(4,128)S(1)} %copy.9.refs_1_, f32[1280,128]{1,0:T(8,128)S(1)} %bitcast.5, s32[3,512]{1,0:T(4,128)S(1)} %copy-done.3, f32[3,512]{1,0:T(4,128)S(1)} %copy-done.4, f32[3,80,512]{2,1,0:T(8,128)S(1)} %copy-done, f32[3,512]{1,0:T(4,128)S(1)} %copy-done.5, ...), custom_call_target="tpu_custom_call" | custom-call | tf_op jit(solution)/shard_map/solve/pallas_call | solution.py:441
  (1 shorter events, 0.0 us)
Async XLA Ops:
  0.0 12.9 %collective-permute-start = (f32[5,4,4,1024]{3,2,1,0:T(4,128)}, f32[5,4,4,1024]{3,2,1,0:T(4,128)S(1)}, u32[]{:S(2)}, u32[]{:S(2)}) collective-permute-start(f32[5,4,4,1024]{3,2,1,0:T(4,128)} %own.1), channel_id=1, source_target_pairs={{0,1},{1,2},{2,3},{3,4},{4,5},{5,6},{6,7},{7,8},{8,9},{9,10},{10,1... | collective-permute-start | bytes 983048 | tf_op jit(solution)/shard_map/ppermute | solution.py:500
  3.9 10.4 %collective-permute-start.1 = (f32[5,4,4,1024]{3,2,1,0:T(4,128)}, f32[5,4,4,1024]{3,2,1,0:T(4,128)S(1)}, u32[]{:S(2)}, u32[]{:S(2)}) collective-permute-start(f32[5,4,4,1024]{3,2,1,0:T(4,128)} %own.1), channel_id=1, source_target_pairs={{1,0},{2,1},{3,2},{4,3},{5,4},{6,5},{7,6},{8,7},{9,8},{10,9},{11,1... | collective-permute-start | bytes 983048 | tf_op jit(solution)/shard_map/ppermute | solution.py:501
  10.0 0.7 copy-start.6
  10.7 1.0 copy-start.1
  11.7 0.7 copy-start.2
  69.1 3.9 %copy-start.7 = (s32[3,2]{0,1:T(2,128)S(1)}, s32[3,2]{0,1:T(2,128)}, u32[]{:S(2)}) copy-start(s32[3,2]{0,1:T(2,128)} %param.10) | copy-start | bytes 76
  69.1 4.0 %copy-start = (f32[3,80,512]{2,1,0:T(8,128)S(1)}, f32[3,80,512]{2,1,0:T(8,128)}, u32[]{:S(2)}) copy-start(f32[3,80,512]{2,1,0:T(8,128)} %refs_5_.3) | copy-start | bytes 1474564
  69.1 21.9 %all-to-all-start.2 = ((f32[16,80,128]{2,1,0:T(8,128)}), f32[16,80,128]{2,1,0:T(8,128)S(1)}, u32[]{:S(2)}, u32[]{:S(2)}) async-start(f32[16,80,128]{2,1,0:T(8,128)} %get-tuple-element.21), calls=%async_computation.2 | async-start | bytes 1310720 | tf_op jit(solution)/shard_map/all_to_all | solution.py:515
  72.9 0.7 copy-start.5
  72.9 0.7 copy-start.4
  72.9 0.7 copy-start.3
